TPU v7x, 1024 devices: a whole 4x8x16 slice. The times are simulated.
1024 devices in a mesh: mp: 16 (over y_hi, x, core), intra: 16 (over z), inter: 4 (over y_lo).
Axes of the slice: x: 4, y: 8 (y_hi: 2, y_lo: 4; y = y_hi * 4 + y_lo), z: 16, core: 2. Of those that a mesh axis runs over, the one named last changes fastest.
Arguments:
- activations: bfloat16 [32768, 512], P(('intra', 'inter'), 'mp'), may hold values from -16 to 16
- cotangent: bfloat16 [32768, 28672], P(('intra', 'inter'), 'mp'), may hold values from -0.03125 to 0.03125
Outputs:
- grad_bucket: float32 [512, 28672], P(('intra', 'inter'), 'mp')
All inputs are finite; a program needn't handle non-finite values.
Results may differ from a plain program's by a relative error of at most 0.0041.
Values may be sent and summed in bfloat16 or wider, within the bound.
No kernel may reach another device: no remote copies, remote signals or barrier semaphores. Data moves between devices by JAX's collectives and lax.ppermute only.
A program may use at most 32 MiB of HBM per device.

v0:
```python
import jax
import jax.numpy as jnp
from jax import lax
from jax.sharding import PartitionSpec as P


def combine_first(pieces):
    return jnp.sum(pieces.astype(jnp.float32), axis=0).astype(jnp.bfloat16)


def combine_second(pieces):
    return jnp.sum(pieces.astype(jnp.float32), axis=0)


def shards(activations, cotangent):
    partial_value = lax.dot_general(
        lax.all_gather(activations, "mp", axis=1, tiled=True),
        cotangent,
        (((0,), (0,)), ((), ())),
        preferred_element_type=jnp.float32,
    )
    terms = partial_value.astype(jnp.bfloat16)
    groups = lax.axis_size("intra")
    replicas = lax.axis_size("inter")
    col_count = terms.shape[1]
    terms = terms.reshape(groups, -1, col_count)
    second_terms = combine_first(
        lax.all_to_all(terms, "intra", split_axis=0, concat_axis=0, tiled=True)
    )
    second_terms = second_terms.reshape(replicas, -1, col_count)
    return combine_second(
        lax.all_to_all(second_terms, "inter", split_axis=0, concat_axis=0, tiled=True)
    )


def solution(mesh):
    return jax.shard_map(
        shards,
        mesh=mesh,
        in_specs=(P(("intra", "inter"), "mp"), P(("intra", "inter"), "mp")),
        out_specs=P(("intra", "inter"), "mp"),
        check_vma=False,
    )
```

profile of v0, /device:TPU:8, one launch (start us, length us, event | category | flops | bytes accessed | tf_op | source)
XLA Modules:
  0.0 151.0 jit_solution(16997535836895850423)
XLA Ops:
  0.0 0.0 copy-start
  0.0 33.0 %all_gather.3 = bf16[512,512]{0,1:T(8,128)(2,1)S(1)} all-gather(bf16[512,32]{0,1:T(8,128)(2,1)} %param.2), channel_id=1, replica_groups=mesh['mp'=16,'intra'=16,'inter'=4] {'mp'}, dimensions={1}, use_global_device_ids=true | all-gather | bytes 557056 | tf_op jit(solution)/shard_map/all_gather | solution.py:17
  33.0 0.0 copy-done
  33.0 1.1 convolution_convert_fusion
  34.1 105.4 %all_to_all.10 = bf16[16,32,1792]{2,1,0:T(8,128)(2,1)} all-to-all(bf16[16,32,1792]{2,1,0:T(8,128)(2,1)S(1)} %bitcast.4), channel_id=1, replica_groups=mesh['mp'=16,'intra'=16,'inter'=4] {'intra'}, dimensions={0} | all-to-all | bytes 3670016 | tf_op jit(solution)/shard_map/all_to_all | solution.py:28
  139.5 1.8 %reduce_sum.21 = bf16[32,1792]{1,0:T(8,128)(2,1)S(1)} reduce(bf16[16,32,1792]{2,1,0:T(8,128)(2,1)} %all_to_all.10, bf16[]{:T(256)} %constant.2.clone.1), dimensions={0}, to_apply=%region_0.0 | reduce | flops 860160 | bytes 1949698 | tf_op jit(solution)/shard_map/reduce_sum | solution.py:8
  141.2 9.1 %all_to_all.11 = bf16[4,8,1792]{2,1,0:T(8,128)(2,1)S(1)} all-to-all(bf16[4,8,1792]{2,1,0:T(8,128)(2,1)S(1)} %bitcast.5), channel_id=1, replica_groups=mesh['mp'=16,'intra'=16,'inter'=4] {'inter'}, dimensions={0} | all-to-all | bytes 229376 | tf_op jit(solution)/shard_map/all_to_all | solution.py:32
  150.3 0.6 convert_reduce_fusion
Async XLA Ops:
  0.0 33.0 %copy-start = (bf16[512,1792]{1,0:T(8,128)(2,1)S(1)}, bf16[512,1792]{1,0:T(8,128)(2,1)}, u32[]{:S(2)}) copy-start(bf16[512,1792]{1,0:T(8,128)(2,1)} %param.3) | copy-start | bytes 5505028
where the time goes:
time: 151 us
  blocking collectives  147 us (97%)
  other arithmetic  2.4 us (2%)
    all_to_all x1, blocking collectives, shards(): lax.all_to_all(terms, 'intra', split_axis=0, concat_axis=0, tiled=True)  105 us
    all_gather x1, blocking collectives, shards(): lax.all_gather(activations, 'mp', axis=1, tiled=True)  33 us
    all_to_all x1, blocking collectives, shards(): lax.all_to_all(second_terms, 'inter', split_axis=0, concat_axis=0, tiled=...  9.1 us

commit v1 on v0

v1 whole, which is shorter than its diff:
```python
import jax
import jax.numpy as jnp
from jax import lax
from jax.sharding import PartitionSpec as P

BF = jnp.bfloat16
F32 = jnp.float32


def ring(size, step):
    return [(i, (i + step) % size) for i in range(size)]


def pairs(size):
    one = [(i, i ^ 1) for i in range(size)]
    other = [(i, (i - 1) % size if i % 2 == 0 else (i + 1) % size) for i in range(size)]
    return one, other


def rotated(blocks, shift, axis):
    doubled = jnp.concatenate([blocks, blocks], axis=axis)
    return lax.dynamic_slice_in_dim(doubled, shift, blocks.shape[axis], axis)


def product(rows, columns):
    return lax.dot_general(
        rows, columns, (((1,), (0,)), ((), ())), preferred_element_type=F32
    ).astype(BF)


def gathered(activations):
    size = lax.axis_size("mp")
    half = size // 2
    far = [[i, i + half] for i in range(half)]
    row = [[h * half + 2 * x + c for x in range(half // 2)] for h in range(2) for c in range(2)]
    chip = [[i, i + 1] for i in range(0, size, 2)]
    out = activations.T
    for groups in (far, row, chip):
        out = lax.all_gather(out, "mp", axis_index_groups=groups)
    out = out.transpose(2, 1, 0, 3, 4)
    return out.reshape(-1, out.shape[-1])


def shards(activations, cotangent):
    n, replicas = lax.axis_size("intra"), lax.axis_size("inter")
    z, y = lax.axis_index("intra"), lax.axis_index("inter")
    features = gathered(activations)
    tokens = features.shape[1]
    blocks = features.reshape(n // 2, 2, replicas, -1, tokens).transpose(1, 2, 0, 3, 4)
    blocks = rotated(rotated(blocks, z % 2, 0), y, 1)
    keep, give = (blocks[i].reshape(-1, tokens) for i in range(2))
    cols = cotangent.shape[1]
    half = cols // 2
    sums = []
    for part, perm in zip((cotangent[:, :half], cotangent[:, half:]), pairs(n)):
        other = lax.ppermute(product(give, part), "intra", perm)
        own = product(keep, part)
        sums.append((own.astype(F32) + other.astype(F32)).astype(BF))
    sums = jnp.concatenate(sums, axis=1).reshape(replicas, -1, cols)
    others = [lax.ppermute(sums[k], "inter", ring(replicas, k)) for k in range(1, replicas)]
    total = sums[0].astype(F32)
    for other in others:
        total = total + other.astype(F32)
    total = total.astype(BF).reshape(n // 2, -1, cols)
    total = lax.all_to_all(
        total, "intra", split_axis=0, concat_axis=0, tiled=True,
        axis_index_groups=[list(range(0, n, 2)), list(range(1, n, 2))],
    )
    return jnp.sum(total.astype(F32), axis=0)


def solution(mesh):
    return jax.shard_map(
        shards,
        mesh=mesh,
        in_specs=(P(("intra", "inter"), "mp"), P(("intra", "inter"), "mp")),
        out_specs=P(("intra", "inter"), "mp"),
        check_vma=False,
    )
```

time: 151 us -> 110 us (0.73)
  the two profiles are of different devices: /device:TPU:8 before, /device:TPU:56 now
where the time goes in v1:
time: 110 us
  blocking collectives  49.7 us (45%)
  starting transfers between devices  30.5 us (28%)
  waiting for transfers between devices  25.2 us (23%)
  matrix products  1.76 us (2%)
  other arithmetic  1.24 us (1%)
  local copies, waits for them, and re-layouts  1.11 us (1%)
    all_to_all x1, blocking collectives, shards(): lax.all_to_all(total, 'intra', split_axis=0, concat_axis=0, tiled=True, a...  25.6 us
    all_gather x3, blocking collectives, gathered(): out = lax.all_gather(out, 'mp', axis_index_groups=groups)  24.2 us
    ppermute x2, starting transfers between devices, shards(): other = lax.ppermute(product(give, part), 'intra', perm)  20.7 us
    ppermute x3, waiting for transfers between devices, shards(): lax.ppermute(sums[k], 'inter', ring(replicas, k))  15.1 us
    ppermute x2, waiting for transfers between devices, shards(): other = lax.ppermute(product(give, part), 'intra', perm)  10 us
    ppermute x3, starting transfers between devices, shards(): lax.ppermute(sums[k], 'inter', ring(replicas, k))  9.85 us
  transfers between devices with their start and end apart: 5, of which 4 were waited for; matrix products, arithmetic and copies ran while one was open for 1% of the time, Pallas kernels for 0%

profile of v1, /device:TPU:56, one launch (start us, length us, event | category | flops | bytes accessed | tf_op | source)
XLA Modules:
  0.0 109.7 jit_solution(10881396793013915754)
XLA Ops:
  0.0 9.0 %all-gather = bf16[64,512]{1,0:T(8,128)(2,1)S(1)} all-gather(bf16[32,512]{1,0:T(8,128)(2,1)} %bitcast.25), channel_id=2, replica_groups={{0,512},{64,576},{128,640},{192,704},{256,768},{320,832},{384,896},{448..., dimensions={0}, use_global_device_ids=true | all-gather | bytes 98304 | tf_op jit(solution)/shard_map/all_gather | solution.py:39
  9.0 12.9 %all-gather.1 = bf16[8,32,512]{2,1,0:T(8,128)(2,1)S(1)} all-gather(bf16[2,32,512]{2,1,0:T(8,128)(2,1)S(1)} %bitcast.20), channel_id=3, replica_groups={{0,128,256,384},{64,192,320,448},{512,640,768,896},{576,704,832,960},{1..., dimensions={0}, use_global_device_ids=true | all-gather | bytes 327680 | tf_op jit(solution)/shard_map/all_gather | solution.py:39
  22.0 2.2 %all-gather.2 = bf16[8,2,32,512]{3,2,1,0:T(8,128)(2,1)S(1)} all-gather(bf16[4,2,32,512]{3,2,1,0:T(8,128)(2,1)S(1)} %bitcast.19), channel_id=4, replica_groups={{0,64},{128,192},{256,320},{384,448},{512,576},{640,704},{768,832},{896..., dimensions={0}, use_global_device_ids=true | all-gather | bytes 786432 | tf_op jit(solution)/shard_map/all_gather | solution.py:39
  24.2 0.0 copy-start
  24.2 0.2 fusion.11
  24.4 0.2 fusion.10
  24.7 1.0 copy-done
  25.7 0.4 convolution_convert_fusion.2
  26.1 4.3 %collective-permute-start = (bf16[256,896]{1,0:T(8,128)(2,1)S(1)}, bf16[256,896]{1,0:T(8,128)(2,1)S(1)}, u32[]{:S(2)}, u32[]{:S(2)}) collective-permute-start(bf16[256,896]{1,0:T(8,128)(2,1)S(1)} %convolution_convert_fusion.2), channel_id=1, source_target_pairs={{0,4},{4,0},{8,12},{12,8},{16,20},{20,16},{24,28},{28,24},{32,36},... | collective-permute-start | bytes 1376264 | tf_op jit(solution)/shard_map/ppermute | solution.py:56
  30.4 0.4 convolution_convert_fusion
  30.9 16.4 %collective-permute-start.1 = (bf16[256,896]{1,0:T(8,128)(2,1)S(1)}, bf16[256,896]{1,0:T(8,128)(2,1)S(1)}, u32[]{:S(2)}, u32[]{:S(2)}) collective-permute-start(bf16[256,896]{1,0:T(8,128)(2,1)S(1)} %convolution_convert_fusion), channel_id=1, source_target_pairs={{0,60},{4,8},{8,4},{12,16},{16,12},{20,24},{24,20},{28,32},{32,28}... | collective-permute-start | bytes 1376264 | tf_op jit(solution)/shard_map/ppermute | solution.py:56
  47.3 0.0 collective-permute-done
  47.3 0.4 add_convert_fusion.1
  47.8 10.0 %collective-permute-done.1 = bf16[256,896]{1,0:T(8,128)(2,1)S(1)} collective-permute-done((bf16[256,896]{1,0:T(8,128)(2,1)S(1)}, bf16[256,896]{1,0:T(8,128)(2,1)S(1)}, u32[]{:S(2)}, u32[]{:S(2)}) %collective-permute-start.1) | collective-permute-done | bytes 458784 | tf_op jit(solution)/shard_map/ppermute | solution.py:56
  57.8 0.4 add_convert_fusion
  58.3 0.1 fusion.15
  58.3 4.6 %collective-permute-start.2 = (bf16[64,1792]{1,0:T(8,128)(2,1)S(1)}, bf16[64,1792]{1,0:T(8,128)(2,1)S(1)}, u32[]{:S(2)}, u32[]{:S(2)}) collective-permute-start(bf16[64,1792]{1,0:T(8,128)(2,1)S(1)} %get-tuple-element.5), channel_id=1, source_target_pairs={{0,1},{1,2},{2,3},{3,0},{4,5},{5,6},{6,7},{7,4},{8,9},{9,10},{10,1... | collective-permute-start | bytes 688136 | tf_op jit(solution)/shard_map/ppermute | solution.py:60
  63.0 1.9 %collective-permute-start.4 = (bf16[64,1792]{1,0:T(8,128)(2,1)S(1)}, bf16[64,1792]{1,0:T(8,128)(2,1)S(1)}, u32[]{:S(2)}, u32[]{:S(2)}) collective-permute-start(bf16[64,1792]{1,0:T(8,128)(2,1)S(1)} %get-tuple-element.6), channel_id=1, source_target_pairs={{0,3},{1,0},{2,1},{3,2},{4,7},{5,4},{6,5},{7,6},{8,11},{9,8},{10,9... | collective-permute-start | bytes 688136 | tf_op jit(solution)/shard_map/ppermute | solution.py:60
  64.9 3.3 %collective-permute-start.3 = (bf16[64,1792]{1,0:T(8,128)(2,1)S(1)}, bf16[64,1792]{1,0:T(8,128)(2,1)S(1)}, u32[]{:S(2)}, u32[]{:S(2)}) collective-permute-start(bf16[64,1792]{1,0:T(8,128)(2,1)S(1)} %get-tuple-element.7), channel_id=1, source_target_pairs={{0,2},{1,3},{2,0},{3,1},{4,6},{5,7},{6,4},{7,5},{8,10},{9,11},{10,... | collective-permute-start | bytes 688136 | tf_op jit(solution)/shard_map/ppermute | solution.py:60
  68.2 0.9 collective-permute-done.2
  69.1 6.3 %collective-permute-done.4 = bf16[64,1792]{1,0:T(8,128)(2,1)S(1)} collective-permute-done((bf16[64,1792]{1,0:T(8,128)(2,1)S(1)}, bf16[64,1792]{1,0:T(8,128)(2,1)S(1)}, u32[]{:S(2)}, u32[]{:S(2)}) %collective-permute-start.4) | collective-permute-done | bytes 229408 | tf_op jit(solution)/shard_map/ppermute | solution.py:60
  75.3 8.0 %collective-permute-done.3 = bf16[64,1792]{1,0:T(8,128)(2,1)S(1)} collective-permute-done((bf16[64,1792]{1,0:T(8,128)(2,1)S(1)}, bf16[64,1792]{1,0:T(8,128)(2,1)S(1)}, u32[]{:S(2)}, u32[]{:S(2)}) %collective-permute-start.3) | collective-permute-done | bytes 229408 | tf_op jit(solution)/shard_map/ppermute | solution.py:60
  83.3 0.1 fusion.12
  83.4 25.6 %all_to_all.5 = bf16[8,8,1792]{2,1,0:T(8,128)(2,1)S(1)} all-to-all(bf16[8,8,1792]{2,1,0:T(8,128)(2,1)S(1)} %fusion.12), channel_id=1, replica_groups={{0,8,16,24,32,40,48,56},{4,12,20,28,36,44,52,60},{1,9,17,25,33,41,49,57..., dimensions={0} | all-to-all | bytes 458752 | tf_op jit(solution)/shard_map/all_to_all | solution.py:65
  109.0 0.7 convert_reduce_fusion
  (4 shorter events, 0.1 us)
Async XLA Ops:
  24.2 1.5 %copy-start = (bf16[512,1792]{1,0:T(8,128)(2,1)S(1)}, bf16[512,1792]{1,0:T(8,128)(2,1)}, u32[]{:S(2)}) copy-start(bf16[512,1792]{1,0:T(8,128)(2,1)} %param.3) | copy-start | bytes 5505028
  26.1 21.2 %collective-permute-start = (bf16[256,896]{1,0:T(8,128)(2,1)S(1)}, bf16[256,896]{1,0:T(8,128)(2,1)S(1)}, u32[]{:S(2)}, u32[]{:S(2)}) collective-permute-start(bf16[256,896]{1,0:T(8,128)(2,1)S(1)} %convolution_convert_fusion.2), channel_id=1, source_target_pairs={{0,4},{4,0},{8,12},{12,8},{16,20},{20,16},{24,28},{28,24},{32,36},... | collective-permute-start | bytes 1376264 | tf_op jit(solution)/shard_map/ppermute | solution.py:56
  30.9 26.9 %collective-permute-start.1 = (bf16[256,896]{1,0:T(8,128)(2,1)S(1)}, bf16[256,896]{1,0:T(8,128)(2,1)S(1)}, u32[]{:S(2)}, u32[]{:S(2)}) collective-permute-start(bf16[256,896]{1,0:T(8,128)(2,1)S(1)} %convolution_convert_fusion), channel_id=1, source_target_pairs={{0,60},{4,8},{8,4},{12,16},{16,12},{20,24},{24,20},{28,32},{32,28}... | collective-permute-start | bytes 1376264 | tf_op jit(solution)/shard_map/ppermute | solution.py:56
  58.3 10.7 %collective-permute-start.2 = (bf16[64,1792]{1,0:T(8,128)(2,1)S(1)}, bf16[64,1792]{1,0:T(8,128)(2,1)S(1)}, u32[]{:S(2)}, u32[]{:S(2)}) collective-permute-start(bf16[64,1792]{1,0:T(8,128)(2,1)S(1)} %get-tuple-element.5), channel_id=1, source_target_pairs={{0,1},{1,2},{2,3},{3,0},{4,5},{5,6},{6,7},{7,4},{8,9},{9,10},{10,1... | collective-permute-start | bytes 688136 | tf_op jit(solution)/shard_map/ppermute | solution.py:60
  63.0 12.3 %collective-permute-start.4 = (bf16[64,1792]{1,0:T(8,128)(2,1)S(1)}, bf16[64,1792]{1,0:T(8,128)(2,1)S(1)}, u32[]{:S(2)}, u32[]{:S(2)}) collective-permute-start(bf16[64,1792]{1,0:T(8,128)(2,1)S(1)} %get-tuple-element.6), channel_id=1, source_target_pairs={{0,3},{1,0},{2,1},{3,2},{4,7},{5,4},{6,5},{7,6},{8,11},{9,8},{10,9... | collective-permute-start | bytes 688136 | tf_op jit(solution)/shard_map/ppermute | solution.py:60
  64.9 18.4 %collective-permute-start.3 = (bf16[64,1792]{1,0:T(8,128)(2,1)S(1)}, bf16[64,1792]{1,0:T(8,128)(2,1)S(1)}, u32[]{:S(2)}, u32[]{:S(2)}) collective-permute-start(bf16[64,1792]{1,0:T(8,128)(2,1)S(1)} %get-tuple-element.7), channel_id=1, source_target_pairs={{0,2},{1,3},{2,0},{3,1},{4,6},{5,7},{6,4},{7,5},{8,10},{9,11},{10,... | collective-permute-start | bytes 688136 | tf_op jit(solution)/shard_map/ppermute | solution.py:60

commit v2 on v1

v2 whole, which is shorter than its diff:
```python
import jax
import jax.numpy as jnp
from jax import lax
from jax.sharding import PartitionSpec as P

BF = jnp.bfloat16
F32 = jnp.float32


def ring(size, step):
    return [(i, (i + step) % size) for i in range(size)]


def rotated(blocks, shift, axis):
    doubled = jnp.concatenate([blocks, blocks], axis=axis)
    return lax.dynamic_slice_in_dim(doubled, shift, blocks.shape[axis], axis)


def product(rows, columns):
    return lax.dot_general(
        rows, columns, (((1,), (0,)), ((), ())), preferred_element_type=F32
    ).astype(BF)


def gathered(activations):
    size = lax.axis_size("mp")
    chips = [[i for i in range(size) if i % 2 == core] for core in range(2)]
    pair = [[i, i + 1] for i in range(0, size, 2)]
    own = activations.T
    copies = jnp.broadcast_to(own[None], (size // 2,) + own.shape)
    half = lax.all_to_all(
        copies, "mp", split_axis=0, concat_axis=0, tiled=True, axis_index_groups=chips
    )
    both = lax.all_gather(half, "mp", axis_index_groups=pair)
    return both.swapaxes(0, 1).reshape(-1, own.shape[1])


def shards(activations, cotangent):
    n, replicas = lax.axis_size("intra"), lax.axis_size("inter")
    y = lax.axis_index("inter")
    features = gathered(activations)
    tokens = features.shape[1]
    cols = cotangent.shape[1]
    blocks = features.reshape(n, replicas, -1, tokens).transpose(1, 0, 2, 3)
    blocks = rotated(blocks, y, 0).reshape(replicas, -1, tokens)
    terms = [product(blocks[k], cotangent) for k in range(replicas)]
    others = [lax.ppermute(terms[k], "inter", ring(replicas, k)) for k in (2, 1, 3)]
    total = terms[0].astype(F32)
    for other in others:
        total = total + other.astype(F32)
    total = total.astype(BF).reshape(n, -1, cols)
    total = lax.all_to_all(total, "intra", split_axis=0, concat_axis=0, tiled=True)
    return jnp.sum(total.astype(F32), axis=0)


def solution(mesh):
    return jax.shard_map(
        shards,
        mesh=mesh,
        in_specs=(P(("intra", "inter"), "mp"), P(("intra", "inter"), "mp")),
        out_specs=P(("intra", "inter"), "mp"),
        check_vma=False,
    )
```

time: 110 us -> 118 us (1.073)
  the two profiles are of different devices: /device:TPU:56 before, /device:TPU:64 now
where the time goes in v2:
time: 118 us; the launch traced here: 117 us
  waiting for transfers between devices  46.4 us (39%)
  blocking collectives  45.8 us (39%)
  starting transfers between devices  20.8 us (18%)
  matrix products  1.69 us (1%)
  local copies, waits for them, and re-layouts  1.64 us (1%)
    all_to_all x1, blocking collectives, shards(): lax.all_to_all(total, 'intra', split_axis=0, concat_axis=0, tiled=True)  43.6 us
    ppermute x3, waiting for transfers between devices, shards(): lax.ppermute(terms[k], 'inter', ring(replicas, k))  35.2 us
    ppermute x3, starting transfers between devices, shards(): lax.ppermute(terms[k], 'inter', ring(replicas, k))  11.3 us
    all_to_all x1, waiting for transfers between devices, gathered(): lax.all_to_all(copies, 'mp', split_axis=0, concat_axis=0, tiled=True, axi...  11.2 us
    all_to_all x1, starting transfers between devices, gathered(): lax.all_to_all(copies, 'mp', split_axis=0, concat_axis=0, tiled=True, axi...  9.56 us
  transfers between devices with their start and end apart: 4, of which 3 were waited for; matrix products, arithmetic and copies ran while one was open for 0% of the time, Pallas kernels for 0%

profile of v2, /device:TPU:64, one launch (start us, length us, event | category | flops | bytes accessed | tf_op | source)
XLA Modules:
  0.0 117.3 jit_solution(4601450251761841023)
XLA Ops:
  0.0 0.0 copy-start
  0.0 1.6 %broadcast_in_dim.2 = bf16[8,32,512]{2,1,0:T(8,128)(2,1)} broadcast(bf16[32,512]{1,0:T(8,128)(2,1)} %bitcast.29), dimensions={1,2} | broadcast | bytes 294912 | tf_op jit(solution)/shard_map/broadcast_in_dim | solution.py:30
  1.6 9.6 %all-to-all-start = ((bf16[8,32,512]{2,1,0:T(8,128)(2,1)}), bf16[8,32,512]{2,1,0:T(8,128)(2,1)S(1)}, u32[]{:S(2)}, u32[]{:S(2)}) async-start(bf16[8,32,512]{2,1,0:T(8,128)(2,1)} %broadcast_in_dim.2), calls=%async_computation | async-start | bytes 524288 | tf_op jit(solution)/shard_map/all_to_all | solution.py:31
  11.2 11.2 %all-to-all-done = bf16[8,32,512]{2,1,0:T(8,128)(2,1)S(1)} async-done(((bf16[8,32,512]{2,1,0:T(8,128)(2,1)}), bf16[8,32,512]{2,1,0:T(8,128)(2,1)S(1)}, u32[]{:S(2)}, u32[]{:S(2)}) %all-to-all-start) | async-done | bytes 262176 | tf_op jit(solution)/shard_map/all_to_all | solution.py:31
  22.4 2.2 %all-gather = bf16[16,32,512]{2,1,0:T(8,128)(2,1)S(1)} all-gather(bf16[8,32,512]{2,1,0:T(8,128)(2,1)S(1)} %all-to-all-done), channel_id=2, replica_groups={{0,64},{128,192},{256,320},{384,448},{512,576},{640,704},{768,832},{896..., dimensions={0}, use_global_device_ids=true | all-gather | bytes 786432 | tf_op jit(solution)/shard_map/all_gather | solution.py:34
  24.6 0.2 fusion.1
  24.8 0.0 copy-done
  24.8 0.4 convolution_convert_fusion.1
  25.2 0.4 convolution_convert_fusion.2
  25.7 0.4 convolution_convert_fusion
  26.1 3.2 %collective-permute-start.2 = (bf16[128,1792]{1,0:T(8,128)(2,1)S(1)}, bf16[128,1792]{1,0:T(8,128)(2,1)S(1)}, u32[]{:S(2)}, u32[]{:S(2)}) collective-permute-start(bf16[128,1792]{1,0:T(8,128)(2,1)S(1)} %convolution_convert_fusion), channel_id=1, source_target_pairs={{0,3},{1,0},{2,1},{3,2},{4,7},{5,4},{6,5},{7,6},{8,11},{9,8},{10,9... | collective-permute-start | bytes 1376264 | tf_op jit(solution)/shard_map/ppermute | solution.py:47
  29.3 5.1 %collective-permute-start = (bf16[128,1792]{1,0:T(8,128)(2,1)S(1)}, bf16[128,1792]{1,0:T(8,128)(2,1)S(1)}, u32[]{:S(2)}, u32[]{:S(2)}) collective-permute-start(bf16[128,1792]{1,0:T(8,128)(2,1)S(1)} %convolution_convert_fusion.2), channel_id=1, source_target_pairs={{0,2},{1,3},{2,0},{3,1},{4,6},{5,7},{6,4},{7,5},{8,10},{9,11},{10,... | collective-permute-start | bytes 1376264 | tf_op jit(solution)/shard_map/ppermute | solution.py:47
  34.4 2.9 %collective-permute-start.1 = (bf16[128,1792]{1,0:T(8,128)(2,1)S(1)}, bf16[128,1792]{1,0:T(8,128)(2,1)S(1)}, u32[]{:S(2)}, u32[]{:S(2)}) collective-permute-start(bf16[128,1792]{1,0:T(8,128)(2,1)S(1)} %convolution_convert_fusion.1), channel_id=1, source_target_pairs={{0,1},{1,2},{2,3},{3,0},{4,5},{5,6},{6,7},{7,4},{8,9},{9,10},{10,1... | collective-permute-start | bytes 1376264 | tf_op jit(solution)/shard_map/ppermute | solution.py:47
  37.4 4.5 %collective-permute-done.2 = bf16[128,1792]{1,0:T(8,128)(2,1)S(1)} collective-permute-done((bf16[128,1792]{1,0:T(8,128)(2,1)S(1)}, bf16[128,1792]{1,0:T(8,128)(2,1)S(1)}, u32[]{:S(2)}, u32[]{:S(2)}) %collective-permute-start.2) | collective-permute-done | bytes 458784 | tf_op jit(solution)/shard_map/ppermute | solution.py:47
  41.9 30.7 %collective-permute-done = bf16[128,1792]{1,0:T(8,128)(2,1)S(1)} collective-permute-done((bf16[128,1792]{1,0:T(8,128)(2,1)S(1)}, bf16[128,1792]{1,0:T(8,128)(2,1)S(1)}, u32[]{:S(2)}, u32[]{:S(2)}) %collective-permute-start) | collective-permute-done | bytes 458784 | tf_op jit(solution)/shard_map/ppermute | solution.py:47
  72.5 0.0 collective-permute-done.1
  72.5 0.4 fusion.2
  73.0 43.6 %all_to_all.10 = bf16[16,8,1792]{2,1,0:T(8,128)(2,1)S(1)} all-to-all(bf16[16,8,1792]{2,1,0:T(8,128)(2,1)S(1)} %fusion.2), channel_id=1, replica_groups=mesh['mp'=16,'intra'=16,'inter'=4] {'intra'}, dimensions={0} | all-to-all | bytes 917504 | tf_op jit(solution)/shard_map/all_to_all | solution.py:52
  116.6 0.7 convert_reduce_fusion
  (1 shorter events, 0.0 us)
Async XLA Ops:
  0.0 24.8 %copy-start = (bf16[512,1792]{1,0:T(8,128)(2,1)S(1)}, bf16[512,1792]{1,0:T(8,128)(2,1)}, u32[]{:S(2)}) copy-start(bf16[512,1792]{1,0:T(8,128)(2,1)} %param.3) | copy-start | bytes 5505028
  1.6 20.8 %all-to-all-start = ((bf16[8,32,512]{2,1,0:T(8,128)(2,1)}), bf16[8,32,512]{2,1,0:T(8,128)(2,1)S(1)}, u32[]{:S(2)}, u32[]{:S(2)}) async-start(bf16[8,32,512]{2,1,0:T(8,128)(2,1)} %broadcast_in_dim.2), calls=%async_computation | async-start | bytes 524288 | tf_op jit(solution)/shard_map/all_to_all | solution.py:31
  26.1 15.8 %collective-permute-start.2 = (bf16[128,1792]{1,0:T(8,128)(2,1)S(1)}, bf16[128,1792]{1,0:T(8,128)(2,1)S(1)}, u32[]{:S(2)}, u32[]{:S(2)}) collective-permute-start(bf16[128,1792]{1,0:T(8,128)(2,1)S(1)} %convolution_convert_fusion), channel_id=1, source_target_pairs={{0,3},{1,0},{2,1},{3,2},{4,7},{5,4},{6,5},{7,6},{8,11},{9,8},{10,9... | collective-permute-start | bytes 1376264 | tf_op jit(solution)/shard_map/ppermute | solution.py:47
  29.3 43.2 %collective-permute-start = (bf16[128,1792]{1,0:T(8,128)(2,1)S(1)}, bf16[128,1792]{1,0:T(8,128)(2,1)S(1)}, u32[]{:S(2)}, u32[]{:S(2)}) collective-permute-start(bf16[128,1792]{1,0:T(8,128)(2,1)S(1)} %convolution_convert_fusion.2), channel_id=1, source_target_pairs={{0,2},{1,3},{2,0},{3,1},{4,6},{5,7},{6,4},{7,5},{8,10},{9,11},{10,... | collective-permute-start | bytes 1376264 | tf_op jit(solution)/shard_map/ppermute | solution.py:47
  34.4 38.1 %collective-permute-start.1 = (bf16[128,1792]{1,0:T(8,128)(2,1)S(1)}, bf16[128,1792]{1,0:T(8,128)(2,1)S(1)}, u32[]{:S(2)}, u32[]{:S(2)}) collective-permute-start(bf16[128,1792]{1,0:T(8,128)(2,1)S(1)} %convolution_convert_fusion.1), channel_id=1, source_target_pairs={{0,1},{1,2},{2,3},{3,0},{4,5},{5,6},{6,7},{7,4},{8,9},{9,10},{10,1... | collective-permute-start | bytes 1376264 | tf_op jit(solution)/shard_map/ppermute | solution.py:47

commit v3 on v2

--- a/solution.py
+++ b/solution.py
@@ -35,22 +35,48 @@
     return both.swapaxes(0, 1).reshape(-1, own.shape[1])
 
 
+ROUNDS = (
+    ((1, (1, 4, 7, -2, -5)), (-1, (-1, 2, 5, -4, -7)), (2, (8,))),
+    ((3, (6,)), (-3, (-6,))),
+    ((3, (3,)), (-3, (-3,))),
+)
+KEPT = (0, 3, -3, 6, -6)
+
+
 def shards(activations, cotangent):
     n, replicas = lax.axis_size("intra"), lax.axis_size("inter")
-    y = lax.axis_index("inter")
+    z = lax.axis_index("intra")
     features = gathered(activations)
     tokens = features.shape[1]
     cols = cotangent.shape[1]
-    blocks = features.reshape(n, replicas, -1, tokens).transpose(1, 0, 2, 3)
-    blocks = rotated(blocks, y, 0).reshape(replicas, -1, tokens)
-    terms = [product(blocks[k], cotangent) for k in range(replicas)]
-    others = [lax.ppermute(terms[k], "inter", ring(replicas, k)) for k in (2, 1, 3)]
-    total = terms[0].astype(F32)
-    for other in others:
-        total = total + other.astype(F32)
-    total = total.astype(BF).reshape(n, -1, cols)
-    total = lax.all_to_all(total, "intra", split_axis=0, concat_axis=0, tiled=True)
-    return jnp.sum(total.astype(F32), axis=0)
+    blocks = rotated(features.reshape(n, -1, tokens), z, 0)
+
+    def terms(numbers):
+        rows = jnp.concatenate([blocks[k % n] for k in numbers], axis=0)
+        return product(rows, cotangent)
+
+    sums = {}
+    for moves in ROUNDS:
+        if not sums:
+            sent = [terms(numbers) for _, numbers in moves]
+        else:
+            sent = [
+                jnp.concatenate([sums.pop(k).astype(BF) for k in numbers], axis=0)
+                for _, numbers in moves
+            ]
+            sent = lax.optimization_barrier(sent)
+        came = [lax.ppermute(x, "intra", ring(n, s)) for x, (s, _) in zip(sent, moves)]
+        if not sums:
+            own = terms(KEPT).reshape(len(KEPT), -1, cols).astype(F32)
+            sums = {k: own[i] for i, k in enumerate(KEPT)}
+        came = lax.optimization_barrier(came)
+        for x, (s, numbers) in zip(came, moves):
+            x = x.reshape(len(numbers), -1, cols).astype(F32)
+            for i, k in enumerate(numbers):
+                sums[k - s] = sums[k - s] + x[i]
+    second = sums[0].astype(BF).reshape(replicas, -1, cols)
+    second = lax.all_to_all(second, "inter", split_axis=0, concat_axis=0, tiled=True)
+    return jnp.sum(second.astype(F32), axis=0)
 
 
 def solution(mesh):

time: 118 us -> 104 us (0.88)
  the two profiles are of different devices: /device:TPU:64 before, /device:TPU:8 now
where the time goes in v3:
time: 104 us
  starting transfers between devices  48.9 us (47%)
  waiting for transfers between devices  39.5 us (38%)
  blocking collectives  10.5 us (10%)
  matrix products  1.81 us (2%)
  local copies, waits for them, and re-layouts  1.7 us (2%)
  other arithmetic  1.21 us (1%)
    ppermute x7, starting transfers between devices, shards(): lax.ppermute(x, 'intra', ring(n, s))  40.2 us
    ppermute x7, waiting for transfers between devices, shards(): lax.ppermute(x, 'intra', ring(n, s))  25.9 us
    all_to_all x1, waiting for transfers between devices, gathered(): lax.all_to_all(copies, 'mp', split_axis=0, concat_axis=0, tiled=True, axi...  13.6 us
    all_to_all x1, starting transfers between devices, gathered(): lax.all_to_all(copies, 'mp', split_axis=0, concat_axis=0, tiled=True, axi...  8.66 us
    all_to_all x1, blocking collectives, shards(): lax.all_to_all(second, 'inter', split_axis=0, concat_axis=0, tiled=True)  8.3 us
    all_gather x1, blocking collectives, gathered(): both = lax.all_gather(half, 'mp', axis_index_groups=pair)  2.17 us
  transfers between devices with their start and end apart: 8, of which 6 were waited for; matrix products, arithmetic and copies ran while one was open for 1% of the time, Pallas kernels for 0%

profile of v3, /device:TPU:8, one launch (start us, length us, event | category | flops | bytes accessed | tf_op | source)
XLA Modules:
  0.0 103.8 jit_solution(7628500154102126670)
XLA Ops:
  0.0 0.0 copy-start
  0.0 1.6 %broadcast_in_dim.2 = bf16[8,32,512]{2,1,0:T(8,128)(2,1)} broadcast(bf16[32,512]{1,0:T(8,128)(2,1)} %bitcast.79), dimensions={1,2} | broadcast | bytes 294912 | tf_op jit(solution)/shard_map/broadcast_in_dim | solution.py:30
  1.6 8.7 %all-to-all-start = ((bf16[8,32,512]{2,1,0:T(8,128)(2,1)}), bf16[8,32,512]{2,1,0:T(8,128)(2,1)S(1)}, u32[]{:S(2)}, u32[]{:S(2)}) async-start(bf16[8,32,512]{2,1,0:T(8,128)(2,1)} %broadcast_in_dim.2), calls=%async_computation | async-start | bytes 524288 | tf_op jit(solution)/shard_map/all_to_all | solution.py:31
  10.3 13.6 %all-to-all-done = bf16[8,32,512]{2,1,0:T(8,128)(2,1)S(1)} async-done(((bf16[8,32,512]{2,1,0:T(8,128)(2,1)}), bf16[8,32,512]{2,1,0:T(8,128)(2,1)S(1)}, u32[]{:S(2)}, u32[]{:S(2)}) %all-to-all-start) | async-done | bytes 262176 | tf_op jit(solution)/shard_map/all_to_all | solution.py:31
  23.9 2.2 %all-gather = bf16[16,32,512]{2,1,0:T(8,128)(2,1)S(1)} all-gather(bf16[8,32,512]{2,1,0:T(8,128)(2,1)S(1)} %all-to-all-done), channel_id=2, replica_groups={{0,64},{128,192},{256,320},{384,448},{512,576},{640,704},{768,832},{896..., dimensions={0}, use_global_device_ids=true | all-gather | bytes 786432 | tf_op jit(solution)/shard_map/all_gather | solution.py:34
  26.1 0.2 fusion.1
  26.4 0.0 copy-done
  26.4 0.5 convolution_convert_fusion.1
  26.9 4.3 %collective-permute-start = (bf16[160,1792]{1,0:T(8,128)(2,1)S(1)}, bf16[160,1792]{1,0:T(8,128)(2,1)S(1)}, u32[]{:S(2)}, u32[]{:S(2)}) collective-permute-start(bf16[160,1792]{1,0:T(8,128)(2,1)S(1)} %convolution_convert_fusion.1), channel_id=1, source_target_pairs={{0,4},{4,8},{8,12},{12,16},{16,20},{20,24},{24,28},{28,32},{32,36}... | collective-permute-start | bytes 1720328 | tf_op jit(solution)/shard_map/ppermute | solution.py:68
  31.2 0.5 convolution_convert_fusion
  31.7 15.9 %collective-permute-start.1 = (bf16[160,1792]{1,0:T(8,128)(2,1)S(1)}, bf16[160,1792]{1,0:T(8,128)(2,1)S(1)}, u32[]{:S(2)}, u32[]{:S(2)}) collective-permute-start(bf16[160,1792]{1,0:T(8,128)(2,1)S(1)} %convolution_convert_fusion), channel_id=1, source_target_pairs={{0,60},{4,0},{8,4},{12,8},{16,12},{20,16},{24,20},{28,24},{32,28},... | collective-permute-start | bytes 1720328 | tf_op jit(solution)/shard_map/ppermute | solution.py:68
  47.5 0.4 convolution_convert_fusion.3
  47.9 1.9 %collective-permute-start.2 = (bf16[32,1792]{1,0:T(8,128)(2,1)S(1)}, bf16[32,1792]{1,0:T(8,128)(2,1)S(1)}, u32[]{:S(2)}, u32[]{:S(2)}) collective-permute-start(bf16[32,1792]{1,0:T(8,128)(2,1)S(1)} %convolution_convert_fusion.3), channel_id=1, source_target_pairs={{0,8},{4,12},{8,16},{12,20},{16,24},{20,28},{24,32},{28,36},{32,40... | collective-permute-start | bytes 344072 | tf_op jit(solution)/shard_map/ppermute | solution.py:68
  49.9 0.5 fusion
  50.3 12.5 %collective-permute-done.2 = bf16[32,1792]{1,0:T(8,128)(2,1)S(1)} collective-permute-done((bf16[32,1792]{1,0:T(8,128)(2,1)S(1)}, bf16[32,1792]{1,0:T(8,128)(2,1)S(1)}, u32[]{:S(2)}, u32[]{:S(2)}) %collective-permute-start.2) | collective-permute-done | bytes 114720 | tf_op jit(solution)/shard_map/ppermute | solution.py:68
  62.8 0.0 collective-permute-done
  62.8 0.0 collective-permute-done.1
  62.8 0.1 convert_element_type.66
  62.9 0.1 convert_element_type.67
  63.0 0.1 fusion.4
  63.1 1.9 %collective-permute-start.3 = (bf16[32,1792]{1,0:T(8,128)(2,1)S(1)}, bf16[32,1792]{1,0:T(8,128)(2,1)S(1)}, u32[]{:S(2)}, u32[]{:S(2)}) collective-permute-start(bf16[32,1792]{1,0:T(8,128)(2,1)S(1)} %get-tuple-element.19), channel_id=1, source_target_pairs={{0,12},{4,16},{8,20},{12,24},{16,28},{20,32},{24,36},{28,40},{32,4... | collective-permute-start | bytes 344072 | tf_op jit(solution)/shard_map/ppermute | solution.py:68
  65.0 6.9 %collective-permute-start.4 = (bf16[32,1792]{1,0:T(8,128)(2,1)S(1)}, bf16[32,1792]{1,0:T(8,128)(2,1)S(1)}, u32[]{:S(2)}, u32[]{:S(2)}) collective-permute-start(bf16[32,1792]{1,0:T(8,128)(2,1)S(1)} %get-tuple-element.20), channel_id=1, source_target_pairs={{0,52},{4,56},{8,60},{12,0},{16,4},{20,8},{24,12},{28,16},{32,20},... | collective-permute-start | bytes 344072 | tf_op jit(solution)/shard_map/ppermute | solution.py:68
  72.0 5.3 %collective-permute-done.3 = bf16[32,1792]{1,0:T(8,128)(2,1)S(1)} collective-permute-done((bf16[32,1792]{1,0:T(8,128)(2,1)S(1)}, bf16[32,1792]{1,0:T(8,128)(2,1)S(1)}, u32[]{:S(2)}, u32[]{:S(2)}) %collective-permute-start.3) | collective-permute-done | bytes 114720 | tf_op jit(solution)/shard_map/ppermute | solution.py:68
  77.2 1.2 %collective-permute-done.4 = bf16[32,1792]{1,0:T(8,128)(2,1)S(1)} collective-permute-done((bf16[32,1792]{1,0:T(8,128)(2,1)S(1)}, bf16[32,1792]{1,0:T(8,128)(2,1)S(1)}, u32[]{:S(2)}, u32[]{:S(2)}) %collective-permute-start.4) | collective-permute-done | bytes 114720 | tf_op jit(solution)/shard_map/ppermute | solution.py:68
  78.4 0.1 fusion.3
  78.5 3.8 %collective-permute-start.5 = (bf16[32,1792]{1,0:T(8,128)(2,1)S(1)}, bf16[32,1792]{1,0:T(8,128)(2,1)S(1)}, u32[]{:S(2)}, u32[]{:S(2)}) collective-permute-start(bf16[32,1792]{1,0:T(8,128)(2,1)S(1)} %get-tuple-element.23), channel_id=1, source_target_pairs={{0,12},{4,16},{8,20},{12,24},{16,28},{20,32},{24,36},{28,40},{32,4... | collective-permute-start | bytes 344072 | tf_op jit(solution)/shard_map/ppermute | solution.py:68
  82.3 5.5 %collective-permute-start.6 = (bf16[32,1792]{1,0:T(8,128)(2,1)S(1)}, bf16[32,1792]{1,0:T(8,128)(2,1)S(1)}, u32[]{:S(2)}, u32[]{:S(2)}) collective-permute-start(bf16[32,1792]{1,0:T(8,128)(2,1)S(1)} %get-tuple-element.24), channel_id=1, source_target_pairs={{0,52},{4,56},{8,60},{12,0},{16,4},{20,8},{24,12},{28,16},{32,20},... | collective-permute-start | bytes 344072 | tf_op jit(solution)/shard_map/ppermute | solution.py:68
  87.8 4.7 %collective-permute-done.5 = bf16[32,1792]{1,0:T(8,128)(2,1)S(1)} collective-permute-done((bf16[32,1792]{1,0:T(8,128)(2,1)S(1)}, bf16[32,1792]{1,0:T(8,128)(2,1)S(1)}, u32[]{:S(2)}, u32[]{:S(2)}) %collective-permute-start.5) | collective-permute-done | bytes 114720 | tf_op jit(solution)/shard_map/ppermute | solution.py:68
  92.6 2.2 %collective-permute-done.6 = bf16[32,1792]{1,0:T(8,128)(2,1)S(1)} collective-permute-done((bf16[32,1792]{1,0:T(8,128)(2,1)S(1)}, bf16[32,1792]{1,0:T(8,128)(2,1)S(1)}, u32[]{:S(2)}, u32[]{:S(2)}) %collective-permute-start.6) | collective-permute-done | bytes 114720 | tf_op jit(solution)/shard_map/ppermute | solution.py:68
  94.8 0.1 fusion.12
  94.8 8.3 %all_to_all.10 = bf16[4,8,1792]{2,1,0:T(8,128)(2,1)S(1)} all-to-all(bf16[4,8,1792]{2,1,0:T(8,128)(2,1)S(1)} %fusion.12), channel_id=1, replica_groups=mesh['mp'=16,'intra'=16,'inter'=4] {'inter'}, dimensions={0} | all-to-all | bytes 229376 | tf_op jit(solution)/shard_map/all_to_all | solution.py:78
  103.1 0.6 convert_reduce_fusion
  (6 shorter events, 0.1 us)
Async XLA Ops:
  0.0 26.4 %copy-start = (bf16[512,1792]{1,0:T(8,128)(2,1)S(1)}, bf16[512,1792]{1,0:T(8,128)(2,1)}, u32[]{:S(2)}) copy-start(bf16[512,1792]{1,0:T(8,128)(2,1)} %param.3) | copy-start | bytes 5505028
  1.6 22.3 %all-to-all-start = ((bf16[8,32,512]{2,1,0:T(8,128)(2,1)}), bf16[8,32,512]{2,1,0:T(8,128)(2,1)S(1)}, u32[]{:S(2)}, u32[]{:S(2)}) async-start(bf16[8,32,512]{2,1,0:T(8,128)(2,1)} %broadcast_in_dim.2), calls=%async_computation | async-start | bytes 524288 | tf_op jit(solution)/shard_map/all_to_all | solution.py:31
  26.9 35.9 %collective-permute-start = (bf16[160,1792]{1,0:T(8,128)(2,1)S(1)}, bf16[160,1792]{1,0:T(8,128)(2,1)S(1)}, u32[]{:S(2)}, u32[]{:S(2)}) collective-permute-start(bf16[160,1792]{1,0:T(8,128)(2,1)S(1)} %convolution_convert_fusion.1), channel_id=1, source_target_pairs={{0,4},{4,8},{8,12},{12,16},{16,20},{20,24},{24,28},{28,32},{32,36}... | collective-permute-start | bytes 1720328 | tf_op jit(solution)/shard_map/ppermute | solution.py:68
  31.7 31.2 %collective-permute-start.1 = (bf16[160,1792]{1,0:T(8,128)(2,1)S(1)}, bf16[160,1792]{1,0:T(8,128)(2,1)S(1)}, u32[]{:S(2)}, u32[]{:S(2)}) collective-permute-start(bf16[160,1792]{1,0:T(8,128)(2,1)S(1)} %convolution_convert_fusion), channel_id=1, source_target_pairs={{0,60},{4,0},{8,4},{12,8},{16,12},{20,16},{24,20},{28,24},{32,28},... | collective-permute-start | bytes 1720328 | tf_op jit(solution)/shard_map/ppermute | solution.py:68
  47.9 14.9 %collective-permute-start.2 = (bf16[32,1792]{1,0:T(8,128)(2,1)S(1)}, bf16[32,1792]{1,0:T(8,128)(2,1)S(1)}, u32[]{:S(2)}, u32[]{:S(2)}) collective-permute-start(bf16[32,1792]{1,0:T(8,128)(2,1)S(1)} %convolution_convert_fusion.3), channel_id=1, source_target_pairs={{0,8},{4,12},{8,16},{12,20},{16,24},{20,28},{24,32},{28,36},{32,40... | collective-permute-start | bytes 344072 | tf_op jit(solution)/shard_map/ppermute | solution.py:68
  63.1 14.2 %collective-permute-start.3 = (bf16[32,1792]{1,0:T(8,128)(2,1)S(1)}, bf16[32,1792]{1,0:T(8,128)(2,1)S(1)}, u32[]{:S(2)}, u32[]{:S(2)}) collective-permute-start(bf16[32,1792]{1,0:T(8,128)(2,1)S(1)} %get-tuple-element.19), channel_id=1, source_target_pairs={{0,12},{4,16},{8,20},{12,24},{16,28},{20,32},{24,36},{28,40},{32,4... | collective-permute-start | bytes 344072 | tf_op jit(solution)/shard_map/ppermute | solution.py:68
  65.0 13.4 %collective-permute-start.4 = (bf16[32,1792]{1,0:T(8,128)(2,1)S(1)}, bf16[32,1792]{1,0:T(8,128)(2,1)S(1)}, u32[]{:S(2)}, u32[]{:S(2)}) collective-permute-start(bf16[32,1792]{1,0:T(8,128)(2,1)S(1)} %get-tuple-element.20), channel_id=1, source_target_pairs={{0,52},{4,56},{8,60},{12,0},{16,4},{20,8},{24,12},{28,16},{32,20},... | collective-permute-start | bytes 344072 | tf_op jit(solution)/shard_map/ppermute | solution.py:68
  78.5 14.0 %collective-permute-start.5 = (bf16[32,1792]{1,0:T(8,128)(2,1)S(1)}, bf16[32,1792]{1,0:T(8,128)(2,1)S(1)}, u32[]{:S(2)}, u32[]{:S(2)}) collective-permute-start(bf16[32,1792]{1,0:T(8,128)(2,1)S(1)} %get-tuple-element.23), channel_id=1, source_target_pairs={{0,12},{4,16},{8,20},{12,24},{16,28},{20,32},{24,36},{28,40},{32,4... | collective-permute-start | bytes 344072 | tf_op jit(solution)/shard_map/ppermute | solution.py:68
  82.3 12.5 %collective-permute-start.6 = (bf16[32,1792]{1,0:T(8,128)(2,1)S(1)}, bf16[32,1792]{1,0:T(8,128)(2,1)S(1)}, u32[]{:S(2)}, u32[]{:S(2)}) collective-permute-start(bf16[32,1792]{1,0:T(8,128)(2,1)S(1)} %get-tuple-element.24), channel_id=1, source_target_pairs={{0,52},{4,56},{8,60},{12,0},{16,4},{20,8},{24,12},{28,16},{32,20},... | collective-permute-start | bytes 344072 | tf_op jit(solution)/shard_map/ppermute | solution.py:68

commit v4 on v3

--- a/solution.py
+++ b/solution.py
@@ -43,13 +43,24 @@
 KEPT = (0, 3, -3, 6, -6)
 
 
-def shards(activations, cotangent):
+def moved(block, step):
+    size, n = lax.axis_size("mp"), lax.axis_size("intra")
+    perm = []
+    for m in range(size):
+        way = step if m % 2 == 0 else -step
+        perm += [(m * n + z, m * n + (z + way) % n) for z in range(n)]
+    return lax.ppermute(block, ("mp", "intra"), perm)
+
+
+def reduced(features, cotangent):
     n, replicas = lax.axis_size("intra"), lax.axis_size("inter")
-    z = lax.axis_index("intra")
-    features = gathered(activations)
+    z, core = lax.axis_index("intra"), lax.axis_index("mp") % 2
     tokens = features.shape[1]
     cols = cotangent.shape[1]
-    blocks = rotated(features.reshape(n, -1, tokens), z, 0)
+    blocks = features.reshape(n, -1, tokens)
+    backward = jnp.concatenate([blocks[:1], blocks[:0:-1]], axis=0)
+    blocks = jnp.where(core == 0, blocks, backward)
+    blocks = rotated(blocks, jnp.where(core == 0, z, (n - z) % n), 0)
 
     def terms(numbers):
         rows = jnp.concatenate([blocks[k % n] for k in numbers], axis=0)
@@ -65,7 +76,7 @@
                 for _, numbers in moves
             ]
             sent = lax.optimization_barrier(sent)
-        came = [lax.ppermute(x, "intra", ring(n, s)) for x, (s, _) in zip(sent, moves)]
+        came = [moved(x, s) for x, (s, _) in zip(sent, moves)]
         if not sums:
             own = terms(KEPT).reshape(len(KEPT), -1, cols).astype(F32)
             sums = {k: own[i] for i, k in enumerate(KEPT)}
@@ -79,6 +90,10 @@
     return jnp.sum(second.astype(F32), axis=0)
 
 
+def shards(activations, cotangent):
+    return reduced(gathered(activations), cotangent)
+
+
 def solution(mesh):
     return jax.shard_map(
         shards,

time: 104 us -> 101 us (0.971)
  the two profiles are of different devices: /device:TPU:8 before, /device:TPU:1 now
where the time goes in v4:
time: 101 us
  starting transfers between devices  41.1 us (41%)
  waiting for transfers between devices  35.5 us (35%)
  blocking collectives  19.3 us (19%)
  matrix products  1.81 us (2%)
  local copies, waits for them, and re-layouts  1.78 us (2%)
  other arithmetic  1.31 us (1%)
    ppermute x7, starting transfers between devices, moved(): return lax.ppermute(block, ('mp', 'intra'), perm)  31 us
    ppermute x7, waiting for transfers between devices, moved(): return lax.ppermute(block, ('mp', 'intra'), perm)  25.4 us
    all_gather x1, blocking collectives, gathered(): both = lax.all_gather(half, 'mp', axis_index_groups=pair)  10.2 us
    all_to_all x1, starting transfers between devices, gathered(): lax.all_to_all(copies, 'mp', split_axis=0, concat_axis=0, tiled=True, axi...  10.1 us
    all_to_all x1, waiting for transfers between devices, gathered(): lax.all_to_all(copies, 'mp', split_axis=0, concat_axis=0, tiled=True, axi...  10.1 us
    all_to_all x1, blocking collectives, reduced(): lax.all_to_all(second, 'inter', split_axis=0, concat_axis=0, tiled=True)  9.04 us
  transfers between devices with their start and end apart: 8, of which 6 were waited for; matrix products, arithmetic and copies ran while one was open for 1% of the time, Pallas kernels for 0%

profile of v4, /device:TPU:1, one launch (start us, length us, event | category | flops | bytes accessed | tf_op | source)
XLA Modules:
  0.0 101.0 jit_solution(10957867984161749913)
XLA Ops:
  0.0 0.0 copy-start
  0.0 1.6 %broadcast_in_dim.2 = bf16[8,32,512]{2,1,0:T(8,128)(2,1)} broadcast(bf16[32,512]{1,0:T(8,128)(2,1)} %bitcast.81), dimensions={1,2} | broadcast | bytes 294912 | tf_op jit(solution)/shard_map/broadcast_in_dim | solution.py:30
  1.6 10.1 %all-to-all-start = ((bf16[8,32,512]{2,1,0:T(8,128)(2,1)}), bf16[8,32,512]{2,1,0:T(8,128)(2,1)S(1)}, u32[]{:S(2)}, u32[]{:S(2)}) async-start(bf16[8,32,512]{2,1,0:T(8,128)(2,1)} %broadcast_in_dim.2), calls=%async_computation | async-start | bytes 524288 | tf_op jit(solution)/shard_map/all_to_all | solution.py:31
  11.7 10.1 %all-to-all-done = bf16[8,32,512]{2,1,0:T(8,128)(2,1)S(1)} async-done(((bf16[8,32,512]{2,1,0:T(8,128)(2,1)}), bf16[8,32,512]{2,1,0:T(8,128)(2,1)S(1)}, u32[]{:S(2)}, u32[]{:S(2)}) %all-to-all-start) | async-done | bytes 262176 | tf_op jit(solution)/shard_map/all_to_all | solution.py:31
  21.8 10.2 %all-gather = bf16[16,32,512]{2,1,0:T(8,128)(2,1)S(1)} all-gather(bf16[8,32,512]{2,1,0:T(8,128)(2,1)S(1)} %all-to-all-done), channel_id=2, replica_groups={{0,64},{128,192},{256,320},{384,448},{512,576},{640,704},{768,832},{896..., dimensions={0}, use_global_device_ids=true | all-gather | bytes 786432 | tf_op jit(solution)/shard_map/all_gather | solution.py:34
  32.2 0.1 maximum_select_fusion
  32.3 0.2 fusion.1
  32.6 0.5 convolution_convert_fusion.1
  33.1 11.6 %collective-permute-start = (bf16[160,1792]{1,0:T(8,128)(2,1)S(1)}, bf16[160,1792]{1,0:T(8,128)(2,1)S(1)}, u32[]{:S(2)}, u32[]{:S(2)}) collective-permute-start(bf16[160,1792]{1,0:T(8,128)(2,1)S(1)} %convolution_convert_fusion.1), channel_id=1, source_target_pairs={{0,4},{4,8},{8,12},{12,16},{16,20},{20,24},{24,28},{28,32},{32,36}... | collective-permute-start | bytes 1720328 | tf_op jit(solution)/shard_map/ppermute | solution.py:52
  44.7 0.5 convolution_convert_fusion
  45.2 1.9 %collective-permute-start.1 = (bf16[160,1792]{1,0:T(8,128)(2,1)S(1)}, bf16[160,1792]{1,0:T(8,128)(2,1)S(1)}, u32[]{:S(2)}, u32[]{:S(2)}) collective-permute-start(bf16[160,1792]{1,0:T(8,128)(2,1)S(1)} %convolution_convert_fusion), channel_id=1, source_target_pairs={{0,60},{4,0},{8,4},{12,8},{16,12},{20,16},{24,20},{28,24},{32,28},... | collective-permute-start | bytes 1720328 | tf_op jit(solution)/shard_map/ppermute | solution.py:52
  47.1 0.4 convolution_convert_fusion.3
  47.5 3.4 %collective-permute-start.2 = (bf16[32,1792]{1,0:T(8,128)(2,1)S(1)}, bf16[32,1792]{1,0:T(8,128)(2,1)S(1)}, u32[]{:S(2)}, u32[]{:S(2)}) collective-permute-start(bf16[32,1792]{1,0:T(8,128)(2,1)S(1)} %convolution_convert_fusion.3), channel_id=1, source_target_pairs={{0,8},{4,12},{8,16},{12,20},{16,24},{20,28},{24,32},{28,36},{32,40... | collective-permute-start | bytes 344072 | tf_op jit(solution)/shard_map/ppermute | solution.py:52
  50.9 0.5 fusion
  51.4 6.5 %collective-permute-done.2 = bf16[32,1792]{1,0:T(8,128)(2,1)S(1)} collective-permute-done((bf16[32,1792]{1,0:T(8,128)(2,1)S(1)}, bf16[32,1792]{1,0:T(8,128)(2,1)S(1)}, u32[]{:S(2)}, u32[]{:S(2)}) %collective-permute-start.2) | collective-permute-done | bytes 114720 | tf_op jit(solution)/shard_map/ppermute | solution.py:52
  57.9 0.0 collective-permute-done
  57.9 2.9 %collective-permute-done.1 = bf16[160,1792]{1,0:T(8,128)(2,1)S(1)} collective-permute-done((bf16[160,1792]{1,0:T(8,128)(2,1)S(1)}, bf16[160,1792]{1,0:T(8,128)(2,1)S(1)}, u32[]{:S(2)}, u32[]{:S(2)}) %collective-permute-start.1) | collective-permute-done | bytes 573472 | tf_op jit(solution)/shard_map/ppermute | solution.py:52
  60.8 0.1 convert_element_type.66
  60.9 0.1 convert_element_type.67
  61.0 0.1 fusion.4
  61.1 3.7 %collective-permute-start.3 = (bf16[32,1792]{1,0:T(8,128)(2,1)S(1)}, bf16[32,1792]{1,0:T(8,128)(2,1)S(1)}, u32[]{:S(2)}, u32[]{:S(2)}) collective-permute-start(bf16[32,1792]{1,0:T(8,128)(2,1)S(1)} %get-tuple-element.19), channel_id=1, source_target_pairs={{0,12},{4,16},{8,20},{12,24},{16,28},{20,32},{24,36},{28,40},{32,4... | collective-permute-start | bytes 344072 | tf_op jit(solution)/shard_map/ppermute | solution.py:52
  64.8 3.3 %collective-permute-start.4 = (bf16[32,1792]{1,0:T(8,128)(2,1)S(1)}, bf16[32,1792]{1,0:T(8,128)(2,1)S(1)}, u32[]{:S(2)}, u32[]{:S(2)}) collective-permute-start(bf16[32,1792]{1,0:T(8,128)(2,1)S(1)} %get-tuple-element.20), channel_id=1, source_target_pairs={{0,52},{4,56},{8,60},{12,0},{16,4},{20,8},{24,12},{28,16},{32,20},... | collective-permute-start | bytes 344072 | tf_op jit(solution)/shard_map/ppermute | solution.py:52
  68.2 3.0 %collective-permute-done.3 = bf16[32,1792]{1,0:T(8,128)(2,1)S(1)} collective-permute-done((bf16[32,1792]{1,0:T(8,128)(2,1)S(1)}, bf16[32,1792]{1,0:T(8,128)(2,1)S(1)}, u32[]{:S(2)}, u32[]{:S(2)}) %collective-permute-start.3) | collective-permute-done | bytes 114720 | tf_op jit(solution)/shard_map/ppermute | solution.py:52
  71.2 6.6 %collective-permute-done.4 = bf16[32,1792]{1,0:T(8,128)(2,1)S(1)} collective-permute-done((bf16[32,1792]{1,0:T(8,128)(2,1)S(1)}, bf16[32,1792]{1,0:T(8,128)(2,1)S(1)}, u32[]{:S(2)}, u32[]{:S(2)}) %collective-permute-start.4) | collective-permute-done | bytes 114720 | tf_op jit(solution)/shard_map/ppermute | solution.py:52
  77.8 0.1 fusion.3
  77.9 1.9 %collective-permute-start.5 = (bf16[32,1792]{1,0:T(8,128)(2,1)S(1)}, bf16[32,1792]{1,0:T(8,128)(2,1)S(1)}, u32[]{:S(2)}, u32[]{:S(2)}) collective-permute-start(bf16[32,1792]{1,0:T(8,128)(2,1)S(1)} %get-tuple-element.23), channel_id=1, source_target_pairs={{0,12},{4,16},{8,20},{12,24},{16,28},{20,32},{24,36},{28,40},{32,4... | collective-permute-start | bytes 344072 | tf_op jit(solution)/shard_map/ppermute | solution.py:52
  79.8 5.2 %collective-permute-start.6 = (bf16[32,1792]{1,0:T(8,128)(2,1)S(1)}, bf16[32,1792]{1,0:T(8,128)(2,1)S(1)}, u32[]{:S(2)}, u32[]{:S(2)}) collective-permute-start(bf16[32,1792]{1,0:T(8,128)(2,1)S(1)} %get-tuple-element.24), channel_id=1, source_target_pairs={{0,52},{4,56},{8,60},{12,0},{16,4},{20,8},{24,12},{28,16},{32,20},... | collective-permute-start | bytes 344072 | tf_op jit(solution)/shard_map/ppermute | solution.py:52
  85.0 6.2 %collective-permute-done.5 = bf16[32,1792]{1,0:T(8,128)(2,1)S(1)} collective-permute-done((bf16[32,1792]{1,0:T(8,128)(2,1)S(1)}, bf16[32,1792]{1,0:T(8,128)(2,1)S(1)}, u32[]{:S(2)}, u32[]{:S(2)}) %collective-permute-start.5) | collective-permute-done | bytes 114720 | tf_op jit(solution)/shard_map/ppermute | solution.py:52
  91.3 0.0 collective-permute-done.6
  91.3 0.1 fusion.12
  91.3 9.0 %all_to_all.10 = bf16[4,8,1792]{2,1,0:T(8,128)(2,1)S(1)} all-to-all(bf16[4,8,1792]{2,1,0:T(8,128)(2,1)S(1)} %fusion.12), channel_id=1, replica_groups=mesh['mp'=16,'intra'=16,'inter'=4] {'inter'}, dimensions={0} | all-to-all | bytes 229376 | tf_op jit(solution)/shard_map/all_to_all | solution.py:89
  100.4 0.6 convert_reduce_fusion
  (10 shorter events, 0.2 us)
Async XLA Ops:
  0.0 32.6 %copy-start = (bf16[512,1792]{1,0:T(8,128)(2,1)S(1)}, bf16[512,1792]{1,0:T(8,128)(2,1)}, u32[]{:S(2)}) copy-start(bf16[512,1792]{1,0:T(8,128)(2,1)} %param.3) | copy-start | bytes 5505028
  1.6 20.2 %all-to-all-start = ((bf16[8,32,512]{2,1,0:T(8,128)(2,1)}), bf16[8,32,512]{2,1,0:T(8,128)(2,1)S(1)}, u32[]{:S(2)}, u32[]{:S(2)}) async-start(bf16[8,32,512]{2,1,0:T(8,128)(2,1)} %broadcast_in_dim.2), calls=%async_computation | async-start | bytes 524288 | tf_op jit(solution)/shard_map/all_to_all | solution.py:31
  33.1 24.8 %collective-permute-start = (bf16[160,1792]{1,0:T(8,128)(2,1)S(1)}, bf16[160,1792]{1,0:T(8,128)(2,1)S(1)}, u32[]{:S(2)}, u32[]{:S(2)}) collective-permute-start(bf16[160,1792]{1,0:T(8,128)(2,1)S(1)} %convolution_convert_fusion.1), channel_id=1, source_target_pairs={{0,4},{4,8},{8,12},{12,16},{16,20},{20,24},{24,28},{28,32},{32,36}... | collective-permute-start | bytes 1720328 | tf_op jit(solution)/shard_map/ppermute | solution.py:52
  45.2 15.6 %collective-permute-start.1 = (bf16[160,1792]{1,0:T(8,128)(2,1)S(1)}, bf16[160,1792]{1,0:T(8,128)(2,1)S(1)}, u32[]{:S(2)}, u32[]{:S(2)}) collective-permute-start(bf16[160,1792]{1,0:T(8,128)(2,1)S(1)} %convolution_convert_fusion), channel_id=1, source_target_pairs={{0,60},{4,0},{8,4},{12,8},{16,12},{20,16},{24,20},{28,24},{32,28},... | collective-permute-start | bytes 1720328 | tf_op jit(solution)/shard_map/ppermute | solution.py:52
  47.5 10.3 %collective-permute-start.2 = (bf16[32,1792]{1,0:T(8,128)(2,1)S(1)}, bf16[32,1792]{1,0:T(8,128)(2,1)S(1)}, u32[]{:S(2)}, u32[]{:S(2)}) collective-permute-start(bf16[32,1792]{1,0:T(8,128)(2,1)S(1)} %convolution_convert_fusion.3), channel_id=1, source_target_pairs={{0,8},{4,12},{8,16},{12,20},{16,24},{20,28},{24,32},{28,36},{32,40... | collective-permute-start | bytes 344072 | tf_op jit(solution)/shard_map/ppermute | solution.py:52
  61.1 10.1 %collective-permute-start.3 = (bf16[32,1792]{1,0:T(8,128)(2,1)S(1)}, bf16[32,1792]{1,0:T(8,128)(2,1)S(1)}, u32[]{:S(2)}, u32[]{:S(2)}) collective-permute-start(bf16[32,1792]{1,0:T(8,128)(2,1)S(1)} %get-tuple-element.19), channel_id=1, source_target_pairs={{0,12},{4,16},{8,20},{12,24},{16,28},{20,32},{24,36},{28,40},{32,4... | collective-permute-start | bytes 344072 | tf_op jit(solution)/shard_map/ppermute | solution.py:52
  64.8 13.0 %collective-permute-start.4 = (bf16[32,1792]{1,0:T(8,128)(2,1)S(1)}, bf16[32,1792]{1,0:T(8,128)(2,1)S(1)}, u32[]{:S(2)}, u32[]{:S(2)}) collective-permute-start(bf16[32,1792]{1,0:T(8,128)(2,1)S(1)} %get-tuple-element.20), channel_id=1, source_target_pairs={{0,52},{4,56},{8,60},{12,0},{16,4},{20,8},{24,12},{28,16},{32,20},... | collective-permute-start | bytes 344072 | tf_op jit(solution)/shard_map/ppermute | solution.py:52
  77.9 13.3 %collective-permute-start.5 = (bf16[32,1792]{1,0:T(8,128)(2,1)S(1)}, bf16[32,1792]{1,0:T(8,128)(2,1)S(1)}, u32[]{:S(2)}, u32[]{:S(2)}) collective-permute-start(bf16[32,1792]{1,0:T(8,128)(2,1)S(1)} %get-tuple-element.23), channel_id=1, source_target_pairs={{0,12},{4,16},{8,20},{12,24},{16,28},{20,32},{24,36},{28,40},{32,4... | collective-permute-start | bytes 344072 | tf_op jit(solution)/shard_map/ppermute | solution.py:52
  79.8 11.4 %collective-permute-start.6 = (bf16[32,1792]{1,0:T(8,128)(2,1)S(1)}, bf16[32,1792]{1,0:T(8,128)(2,1)S(1)}, u32[]{:S(2)}, u32[]{:S(2)}) collective-permute-start(bf16[32,1792]{1,0:T(8,128)(2,1)S(1)} %get-tuple-element.24), channel_id=1, source_target_pairs={{0,52},{4,56},{8,60},{12,0},{16,4},{20,8},{24,12},{28,16},{32,20},... | collective-permute-start | bytes 344072 | tf_op jit(solution)/shard_map/ppermute | solution.py:52

commit v5 on v4

--- a/solution.py
+++ b/solution.py
@@ -36,11 +36,11 @@
 
 
 ROUNDS = (
-    ((1, (1, 4, 7, -2, -5)), (-1, (-1, 2, 5, -4, -7)), (2, (8,))),
-    ((3, (6,)), (-3, (-6,))),
-    ((3, (3,)), (-3, (-3,))),
+    ((1, (1, 5, 8, -2, -5)), (-1, (-1, 2, 6, -4, -7))),
+    ((3, (3, 7)), (-3, (-6,))),
+    ((4, (4,)), (-3, (-3,))),
 )
-KEPT = (0, 3, -3, 6, -6)
+KEPT = (0, 3, 4, 7, -3, -6)
 
 
 def moved(block, step):

time: 101 us -> 101 us (level)
  the two profiles are of different devices: /device:TPU:1 before, /device:TPU:64 now
where the time goes in v5:
time: 101 us; the launch traced here: 100 us
  starting transfers between devices  44.7 us (44%)
  waiting for transfers between devices  38.1 us (38%)
  blocking collectives  12.7 us (13%)
  local copies, waits for them, and re-layouts  1.78 us (2%)
  matrix products  1.46 us (1%)
  other arithmetic  1.4 us (1%)
    ppermute x6, starting transfers between devices, moved(): return lax.ppermute(block, ('mp', 'intra'), perm)  35.2 us
    ppermute x6, waiting for transfers between devices, moved(): return lax.ppermute(block, ('mp', 'intra'), perm)  26.9 us
    all_to_all x1, waiting for transfers between devices, gathered(): lax.all_to_all(copies, 'mp', split_axis=0, concat_axis=0, tiled=True, axi...  11.2 us
    all_to_all x1, blocking collectives, reduced(): lax.all_to_all(second, 'inter', split_axis=0, concat_axis=0, tiled=True)  10.5 us
    all_to_all x1, starting transfers between devices, gathered(): lax.all_to_all(copies, 'mp', split_axis=0, concat_axis=0, tiled=True, axi...  9.56 us
    all_gather x1, blocking collectives, gathered(): both = lax.all_gather(half, 'mp', axis_index_groups=pair)  2.17 us
  transfers between devices with their start and end apart: 7, of which 6 were waited for; matrix products, arithmetic and copies ran while one was open for 1% of the time, Pallas kernels for 0%

profile of v5, /device:TPU:64, one launch (start us, length us, event | category | flops | bytes accessed | tf_op | source)
XLA Modules:
  0.0 100.4 jit_solution(16442261664720768982)
XLA Ops:
  0.0 0.0 copy-start
  0.0 1.6 %broadcast_in_dim.2 = bf16[8,32,512]{2,1,0:T(8,128)(2,1)} broadcast(bf16[32,512]{1,0:T(8,128)(2,1)} %bitcast.81), dimensions={1,2} | broadcast | bytes 294912 | tf_op jit(solution)/shard_map/broadcast_in_dim | solution.py:30
  1.6 9.6 %all-to-all-start = ((bf16[8,32,512]{2,1,0:T(8,128)(2,1)}), bf16[8,32,512]{2,1,0:T(8,128)(2,1)S(1)}, u32[]{:S(2)}, u32[]{:S(2)}) async-start(bf16[8,32,512]{2,1,0:T(8,128)(2,1)} %broadcast_in_dim.2), calls=%async_computation | async-start | bytes 524288 | tf_op jit(solution)/shard_map/all_to_all | solution.py:31
  11.2 11.2 %all-to-all-done = bf16[8,32,512]{2,1,0:T(8,128)(2,1)S(1)} async-done(((bf16[8,32,512]{2,1,0:T(8,128)(2,1)}), bf16[8,32,512]{2,1,0:T(8,128)(2,1)S(1)}, u32[]{:S(2)}, u32[]{:S(2)}) %all-to-all-start) | async-done | bytes 262176 | tf_op jit(solution)/shard_map/all_to_all | solution.py:31
  22.4 2.2 %all-gather = bf16[16,32,512]{2,1,0:T(8,128)(2,1)S(1)} all-gather(bf16[8,32,512]{2,1,0:T(8,128)(2,1)S(1)} %all-to-all-done), channel_id=2, replica_groups={{0,64},{128,192},{256,320},{384,448},{512,576},{640,704},{768,832},{896..., dimensions={0}, use_global_device_ids=true | all-gather | bytes 786432 | tf_op jit(solution)/shard_map/all_gather | solution.py:34
  24.7 0.1 maximum_select_fusion
  24.8 0.2 fusion.1
  25.2 0.0 copy-done
  25.2 0.5 convolution_convert_fusion.1
  25.6 0.5 convolution_convert_fusion.2
  26.1 4.3 %collective-permute-start = (bf16[160,1792]{1,0:T(8,128)(2,1)S(1)}, bf16[160,1792]{1,0:T(8,128)(2,1)S(1)}, u32[]{:S(2)}, u32[]{:S(2)}) collective-permute-start(bf16[160,1792]{1,0:T(8,128)(2,1)S(1)} %convolution_convert_fusion.2), channel_id=1, source_target_pairs={{0,4},{4,8},{8,12},{12,16},{16,20},{20,24},{24,28},{28,32},{32,36}... | collective-permute-start | bytes 1720328 | tf_op jit(solution)/shard_map/ppermute | solution.py:52
  30.4 5.5 %collective-permute-start.1 = (bf16[160,1792]{1,0:T(8,128)(2,1)S(1)}, bf16[160,1792]{1,0:T(8,128)(2,1)S(1)}, u32[]{:S(2)}, u32[]{:S(2)}) collective-permute-start(bf16[160,1792]{1,0:T(8,128)(2,1)S(1)} %convolution_convert_fusion.1), channel_id=1, source_target_pairs={{0,60},{4,0},{8,4},{12,8},{16,12},{20,16},{24,20},{28,24},{32,28},... | collective-permute-start | bytes 1720328 | tf_op jit(solution)/shard_map/ppermute | solution.py:52
  36.0 0.5 fusion
  36.5 5.2 %collective-permute-done = bf16[160,1792]{1,0:T(8,128)(2,1)S(1)} collective-permute-done((bf16[160,1792]{1,0:T(8,128)(2,1)S(1)}, bf16[160,1792]{1,0:T(8,128)(2,1)S(1)}, u32[]{:S(2)}, u32[]{:S(2)}) %collective-permute-start) | collective-permute-done | bytes 573472 | tf_op jit(solution)/shard_map/ppermute | solution.py:52
  41.7 4.8 %collective-permute-done.1 = bf16[160,1792]{1,0:T(8,128)(2,1)S(1)} collective-permute-done((bf16[160,1792]{1,0:T(8,128)(2,1)S(1)}, bf16[160,1792]{1,0:T(8,128)(2,1)S(1)}, u32[]{:S(2)}, u32[]{:S(2)}) %collective-permute-start.1) | collective-permute-done | bytes 573472 | tf_op jit(solution)/shard_map/ppermute | solution.py:52
  46.5 0.1 convert_element_type.61
  46.6 0.1 convert_element_type.62
  46.7 0.1 fusion.8
  46.8 6.5 %collective-permute-start.2 = (bf16[64,1792]{1,0:T(8,128)(2,1)S(1)}, bf16[64,1792]{1,0:T(8,128)(2,1)S(1)}, u32[]{:S(2)}, u32[]{:S(2)}) collective-permute-start(bf16[64,1792]{1,0:T(8,128)(2,1)S(1)} %pad_maximum_fusion), channel_id=1, source_target_pairs={{0,12},{4,16},{8,20},{12,24},{16,28},{20,32},{24,36},{28,40},{32,4... | collective-permute-start | bytes 688136 | tf_op jit(solution)/shard_map/ppermute | solution.py:52
  53.4 9.2 %collective-permute-start.3 = (bf16[32,1792]{1,0:T(8,128)(2,1)S(1)}, bf16[32,1792]{1,0:T(8,128)(2,1)S(1)}, u32[]{:S(2)}, u32[]{:S(2)}) collective-permute-start(bf16[32,1792]{1,0:T(8,128)(2,1)S(1)} %get-tuple-element.18), channel_id=1, source_target_pairs={{0,52},{4,56},{8,60},{12,0},{16,4},{20,8},{24,12},{28,16},{32,20},... | collective-permute-start | bytes 344072 | tf_op jit(solution)/shard_map/ppermute | solution.py:52
  62.5 9.9 %collective-permute-done.3 = bf16[32,1792]{1,0:T(8,128)(2,1)S(1)} collective-permute-done((bf16[32,1792]{1,0:T(8,128)(2,1)S(1)}, bf16[32,1792]{1,0:T(8,128)(2,1)S(1)}, u32[]{:S(2)}, u32[]{:S(2)}) %collective-permute-start.3) | collective-permute-done | bytes 114720 | tf_op jit(solution)/shard_map/ppermute | solution.py:52
  72.4 0.0 collective-permute-done.2
  72.5 0.1 fusion.3
  72.5 4.1 %collective-permute-start.4 = (bf16[32,1792]{1,0:T(8,128)(2,1)S(1)}, bf16[32,1792]{1,0:T(8,128)(2,1)S(1)}, u32[]{:S(2)}, u32[]{:S(2)}) collective-permute-start(bf16[32,1792]{1,0:T(8,128)(2,1)S(1)} %get-tuple-element.21), channel_id=1, source_target_pairs={{0,16},{4,20},{8,24},{12,28},{16,32},{20,36},{24,40},{28,44},{32,4... | collective-permute-start | bytes 344072 | tf_op jit(solution)/shard_map/ppermute | solution.py:52
  76.6 5.6 %collective-permute-start.5 = (bf16[32,1792]{1,0:T(8,128)(2,1)S(1)}, bf16[32,1792]{1,0:T(8,128)(2,1)S(1)}, u32[]{:S(2)}, u32[]{:S(2)}) collective-permute-start(bf16[32,1792]{1,0:T(8,128)(2,1)S(1)} %get-tuple-element.22), channel_id=1, source_target_pairs={{0,52},{4,56},{8,60},{12,0},{16,4},{20,8},{24,12},{28,16},{32,20},... | collective-permute-start | bytes 344072 | tf_op jit(solution)/shard_map/ppermute | solution.py:52
  82.2 3.5 %collective-permute-done.4 = bf16[32,1792]{1,0:T(8,128)(2,1)S(1)} collective-permute-done((bf16[32,1792]{1,0:T(8,128)(2,1)S(1)}, bf16[32,1792]{1,0:T(8,128)(2,1)S(1)}, u32[]{:S(2)}, u32[]{:S(2)}) %collective-permute-start.4) | collective-permute-done | bytes 114720 | tf_op jit(solution)/shard_map/ppermute | solution.py:52
  85.7 3.4 %collective-permute-done.5 = bf16[32,1792]{1,0:T(8,128)(2,1)S(1)} collective-permute-done((bf16[32,1792]{1,0:T(8,128)(2,1)S(1)}, bf16[32,1792]{1,0:T(8,128)(2,1)S(1)}, u32[]{:S(2)}, u32[]{:S(2)}) %collective-permute-start.5) | collective-permute-done | bytes 114720 | tf_op jit(solution)/shard_map/ppermute | solution.py:52
  89.1 0.1 fusion.11
  89.2 10.5 %all_to_all.10 = bf16[4,8,1792]{2,1,0:T(8,128)(2,1)S(1)} all-to-all(bf16[4,8,1792]{2,1,0:T(8,128)(2,1)S(1)} %fusion.11), channel_id=1, replica_groups=mesh['mp'=16,'intra'=16,'inter'=4] {'inter'}, dimensions={0} | all-to-all | bytes 229376 | tf_op jit(solution)/shard_map/all_to_all | solution.py:89
  99.8 0.6 convert_reduce_fusion
  (13 shorter events, 0.2 us)
Async XLA Ops:
  0.0 25.2 %copy-start = (bf16[512,1792]{1,0:T(8,128)(2,1)S(1)}, bf16[512,1792]{1,0:T(8,128)(2,1)}, u32[]{:S(2)}) copy-start(bf16[512,1792]{1,0:T(8,128)(2,1)} %param.3) | copy-start | bytes 5505028
  1.6 20.8 %all-to-all-start = ((bf16[8,32,512]{2,1,0:T(8,128)(2,1)}), bf16[8,32,512]{2,1,0:T(8,128)(2,1)S(1)}, u32[]{:S(2)}, u32[]{:S(2)}) async-start(bf16[8,32,512]{2,1,0:T(8,128)(2,1)} %broadcast_in_dim.2), calls=%async_computation | async-start | bytes 524288 | tf_op jit(solution)/shard_map/all_to_all | solution.py:31
  26.1 15.6 %collective-permute-start = (bf16[160,1792]{1,0:T(8,128)(2,1)S(1)}, bf16[160,1792]{1,0:T(8,128)(2,1)S(1)}, u32[]{:S(2)}, u32[]{:S(2)}) collective-permute-start(bf16[160,1792]{1,0:T(8,128)(2,1)S(1)} %convolution_convert_fusion.2), channel_id=1, source_target_pairs={{0,4},{4,8},{8,12},{12,16},{16,20},{20,24},{24,28},{28,32},{32,36}... | collective-permute-start | bytes 1720328 | tf_op jit(solution)/shard_map/ppermute | solution.py:52
  30.4 16.1 %collective-permute-start.1 = (bf16[160,1792]{1,0:T(8,128)(2,1)S(1)}, bf16[160,1792]{1,0:T(8,128)(2,1)S(1)}, u32[]{:S(2)}, u32[]{:S(2)}) collective-permute-start(bf16[160,1792]{1,0:T(8,128)(2,1)S(1)} %convolution_convert_fusion.1), channel_id=1, source_target_pairs={{0,60},{4,0},{8,4},{12,8},{16,12},{20,16},{24,20},{28,24},{32,28},... | collective-permute-start | bytes 1720328 | tf_op jit(solution)/shard_map/ppermute | solution.py:52
  46.8 25.6 %collective-permute-start.2 = (bf16[64,1792]{1,0:T(8,128)(2,1)S(1)}, bf16[64,1792]{1,0:T(8,128)(2,1)S(1)}, u32[]{:S(2)}, u32[]{:S(2)}) collective-permute-start(bf16[64,1792]{1,0:T(8,128)(2,1)S(1)} %pad_maximum_fusion), channel_id=1, source_target_pairs={{0,12},{4,16},{8,20},{12,24},{16,28},{20,32},{24,36},{28,40},{32,4... | collective-permute-start | bytes 688136 | tf_op jit(solution)/shard_map/ppermute | solution.py:52
  53.4 19.1 %collective-permute-start.3 = (bf16[32,1792]{1,0:T(8,128)(2,1)S(1)}, bf16[32,1792]{1,0:T(8,128)(2,1)S(1)}, u32[]{:S(2)}, u32[]{:S(2)}) collective-permute-start(bf16[32,1792]{1,0:T(8,128)(2,1)S(1)} %get-tuple-element.18), channel_id=1, source_target_pairs={{0,52},{4,56},{8,60},{12,0},{16,4},{20,8},{24,12},{28,16},{32,20},... | collective-permute-start | bytes 344072 | tf_op jit(solution)/shard_map/ppermute | solution.py:52
  72.5 13.2 %collective-permute-start.4 = (bf16[32,1792]{1,0:T(8,128)(2,1)S(1)}, bf16[32,1792]{1,0:T(8,128)(2,1)S(1)}, u32[]{:S(2)}, u32[]{:S(2)}) collective-permute-start(bf16[32,1792]{1,0:T(8,128)(2,1)S(1)} %get-tuple-element.21), channel_id=1, source_target_pairs={{0,16},{4,20},{8,24},{12,28},{16,32},{20,36},{24,40},{28,44},{32,4... | collective-permute-start | bytes 344072 | tf_op jit(solution)/shard_map/ppermute | solution.py:52
  76.6 12.5 %collective-permute-start.5 = (bf16[32,1792]{1,0:T(8,128)(2,1)S(1)}, bf16[32,1792]{1,0:T(8,128)(2,1)S(1)}, u32[]{:S(2)}, u32[]{:S(2)}) collective-permute-start(bf16[32,1792]{1,0:T(8,128)(2,1)S(1)} %get-tuple-element.22), channel_id=1, source_target_pairs={{0,52},{4,56},{8,60},{12,0},{16,4},{20,8},{24,12},{28,16},{32,20},... | collective-permute-start | bytes 344072 | tf_op jit(solution)/shard_map/ppermute | solution.py:52

commit v6 on v5

--- a/solution.py
+++ b/solution.py
@@ -24,15 +24,18 @@
 
 def gathered(activations):
     size = lax.axis_size("mp")
-    chips = [[i for i in range(size) if i % 2 == core] for core in range(2)]
+    half = size // 2
+    far = [[i, i + half] for i in range(half)]
+    line = [[f * half + i + c for i in range(0, half, 2)] for f in range(2) for c in range(2)]
     pair = [[i, i + 1] for i in range(0, size, 2)]
     own = activations.T
-    copies = jnp.broadcast_to(own[None], (size // 2,) + own.shape)
-    half = lax.all_to_all(
-        copies, "mp", split_axis=0, concat_axis=0, tiled=True, axis_index_groups=chips
+    out = lax.all_gather(own, "mp", axis_index_groups=far)
+    out = jnp.broadcast_to(out[None], (half // 2,) + out.shape)
+    out = lax.all_to_all(
+        out, "mp", split_axis=0, concat_axis=0, tiled=True, axis_index_groups=line
     )
-    both = lax.all_gather(half, "mp", axis_index_groups=pair)
-    return both.swapaxes(0, 1).reshape(-1, own.shape[1])
+    out = lax.all_gather(out, "mp", axis_index_groups=pair)
+    return out.transpose(2, 1, 0, 3, 4).reshape(-1, own.shape[1])
 
 
 ROUNDS = (

time: 101 us -> 99.2 us (0.982)
  the two profiles are of different devices: /device:TPU:64 before, /device:TPU:56 now
where the time goes in v6:
time: 99.2 us; the launch traced here: 97.3 us
  starting transfers between devices  42.8 us (43%)
  waiting for transfers between devices  30.7 us (31%)
  blocking collectives  19.8 us (20%)
  matrix products  1.46 us (1%)
  other arithmetic  1.4 us (1%)
    ppermute x6, starting transfers between devices, moved(): return lax.ppermute(block, ('mp', 'intra'), perm)  38.5 us
    ppermute x6, waiting for transfers between devices, moved(): return lax.ppermute(block, ('mp', 'intra'), perm)  24 us
    all_gather x1, blocking collectives, gathered(): out = lax.all_gather(own, 'mp', axis_index_groups=far)  9.18 us
    all_to_all x1, blocking collectives, reduced(): lax.all_to_all(second, 'inter', split_axis=0, concat_axis=0, tiled=True)  8.5 us
    all_to_all x1, waiting for transfers between devices, gathered(): lax.all_to_all(out, 'mp', split_axis=0, concat_axis=0, tiled=True, axis_i...  6.68 us
    all_to_all x1, starting transfers between devices, gathered(): lax.all_to_all(out, 'mp', split_axis=0, concat_axis=0, tiled=True, axis_i...  4.29 us
    all_gather x1, blocking collectives, gathered(): out = lax.all_gather(out, 'mp', axis_index_groups=pair)  2.17 us
  transfers between devices with their start and end apart: 7, of which 7 were waited for; matrix products, arithmetic and copies ran while one was open for 1% of the time, Pallas kernels for 0%

profile of v6, /device:TPU:56, one launch (start us, length us, event | category | flops | bytes accessed | tf_op | source)
XLA Modules:
  0.0 97.3 jit_solution(10862002352591893949)
XLA Ops:
  0.0 0.0 copy-start
  0.0 9.2 %all-gather = bf16[64,512]{1,0:T(8,128)(2,1)S(1)} all-gather(bf16[32,512]{1,0:T(8,128)(2,1)} %bitcast.83), channel_id=2, replica_groups={{0,512},{64,576},{128,640},{192,704},{256,768},{320,832},{384,896},{448..., dimensions={0}, use_global_device_ids=true | all-gather | bytes 98304 | tf_op jit(solution)/shard_map/all_gather | solution.py:32
  9.2 0.7 broadcast_in_dim.2
  9.9 4.3 %all-to-all-start = ((bf16[4,2,32,512]{3,2,1,0:T(8,128)(2,1)}), bf16[4,2,32,512]{3,2,1,0:T(8,128)(2,1)S(1)}, u32[]{:S(2)}, u32[]{:S(2)}) async-start(bf16[4,2,32,512]{3,2,1,0:T(8,128)(2,1)} %broadcast_in_dim.2), calls=%async_computation | async-start | bytes 524288 | tf_op jit(solution)/shard_map/all_to_all | solution.py:34
  14.2 6.7 %all-to-all-done = bf16[4,2,32,512]{3,2,1,0:T(8,128)(2,1)S(1)} async-done(((bf16[4,2,32,512]{3,2,1,0:T(8,128)(2,1)}), bf16[4,2,32,512]{3,2,1,0:T(8,128)(2,1)S(1)}, u32[]{:S(2)}, u32[]{:S(2)}) %all-to-all-start) | async-done | bytes 262176 | tf_op jit(solution)/shard_map/all_to_all | solution.py:34
  20.9 2.2 %all-gather.1 = bf16[8,2,32,512]{3,2,1,0:T(8,128)(2,1)S(1)} all-gather(bf16[4,2,32,512]{3,2,1,0:T(8,128)(2,1)S(1)} %all-to-all-done), channel_id=3, replica_groups={{0,64},{128,192},{256,320},{384,448},{512,576},{640,704},{768,832},{896..., dimensions={0}, use_global_device_ids=true | all-gather | bytes 786432 | tf_op jit(solution)/shard_map/all_gather | solution.py:37
  23.2 0.1 maximum_select_fusion
  23.3 0.2 fusion.1
  23.6 0.0 copy-done
  23.6 0.5 convolution_convert_fusion.1
  24.1 0.5 convolution_convert_fusion.2
  24.6 4.3 %collective-permute-start = (bf16[160,1792]{1,0:T(8,128)(2,1)S(1)}, bf16[160,1792]{1,0:T(8,128)(2,1)S(1)}, u32[]{:S(2)}, u32[]{:S(2)}) collective-permute-start(bf16[160,1792]{1,0:T(8,128)(2,1)S(1)} %convolution_convert_fusion.2), channel_id=1, source_target_pairs={{0,4},{4,8},{8,12},{12,16},{16,20},{20,24},{24,28},{28,32},{32,36}... | collective-permute-start | bytes 1720328 | tf_op jit(solution)/shard_map/ppermute | solution.py:55
  28.9 15.9 %collective-permute-start.1 = (bf16[160,1792]{1,0:T(8,128)(2,1)S(1)}, bf16[160,1792]{1,0:T(8,128)(2,1)S(1)}, u32[]{:S(2)}, u32[]{:S(2)}) collective-permute-start(bf16[160,1792]{1,0:T(8,128)(2,1)S(1)} %convolution_convert_fusion.1), channel_id=1, source_target_pairs={{0,60},{4,0},{8,4},{12,8},{16,12},{20,16},{24,20},{28,24},{32,28},... | collective-permute-start | bytes 1720328 | tf_op jit(solution)/shard_map/ppermute | solution.py:55
  44.7 0.5 fusion
  45.3 7.3 %collective-permute-done = bf16[160,1792]{1,0:T(8,128)(2,1)S(1)} collective-permute-done((bf16[160,1792]{1,0:T(8,128)(2,1)S(1)}, bf16[160,1792]{1,0:T(8,128)(2,1)S(1)}, u32[]{:S(2)}, u32[]{:S(2)}) %collective-permute-start) | collective-permute-done | bytes 573472 | tf_op jit(solution)/shard_map/ppermute | solution.py:55
  52.5 2.8 %collective-permute-done.1 = bf16[160,1792]{1,0:T(8,128)(2,1)S(1)} collective-permute-done((bf16[160,1792]{1,0:T(8,128)(2,1)S(1)}, bf16[160,1792]{1,0:T(8,128)(2,1)S(1)}, u32[]{:S(2)}, u32[]{:S(2)}) %collective-permute-start.1) | collective-permute-done | bytes 573472 | tf_op jit(solution)/shard_map/ppermute | solution.py:55
  55.3 0.1 convert_element_type.61
  55.4 0.1 convert_element_type.62
  55.5 0.1 fusion.8
  55.6 1.9 %collective-permute-start.2 = (bf16[64,1792]{1,0:T(8,128)(2,1)S(1)}, bf16[64,1792]{1,0:T(8,128)(2,1)S(1)}, u32[]{:S(2)}, u32[]{:S(2)}) collective-permute-start(bf16[64,1792]{1,0:T(8,128)(2,1)S(1)} %pad_maximum_fusion), channel_id=1, source_target_pairs={{0,12},{4,16},{8,20},{12,24},{16,28},{20,32},{24,36},{28,40},{32,4... | collective-permute-start | bytes 688136 | tf_op jit(solution)/shard_map/ppermute | solution.py:55
  57.5 6.9 %collective-permute-start.3 = (bf16[32,1792]{1,0:T(8,128)(2,1)S(1)}, bf16[32,1792]{1,0:T(8,128)(2,1)S(1)}, u32[]{:S(2)}, u32[]{:S(2)}) collective-permute-start(bf16[32,1792]{1,0:T(8,128)(2,1)S(1)} %get-tuple-element.18), channel_id=1, source_target_pairs={{0,52},{4,56},{8,60},{12,0},{16,4},{20,8},{24,12},{28,16},{32,20},... | collective-permute-start | bytes 344072 | tf_op jit(solution)/shard_map/ppermute | solution.py:55
  64.5 4.6 %collective-permute-done.3 = bf16[32,1792]{1,0:T(8,128)(2,1)S(1)} collective-permute-done((bf16[32,1792]{1,0:T(8,128)(2,1)S(1)}, bf16[32,1792]{1,0:T(8,128)(2,1)S(1)}, u32[]{:S(2)}, u32[]{:S(2)}) %collective-permute-start.3) | collective-permute-done | bytes 114720 | tf_op jit(solution)/shard_map/ppermute | solution.py:55
  69.1 3.0 %collective-permute-done.2 = bf16[64,1792]{1,0:T(8,128)(2,1)S(1)} collective-permute-done((bf16[64,1792]{1,0:T(8,128)(2,1)S(1)}, bf16[64,1792]{1,0:T(8,128)(2,1)S(1)}, u32[]{:S(2)}, u32[]{:S(2)}) %collective-permute-start.2) | collective-permute-done | bytes 229408 | tf_op jit(solution)/shard_map/ppermute | solution.py:55
  72.1 0.1 fusion.3
  72.2 2.7 %collective-permute-start.4 = (bf16[32,1792]{1,0:T(8,128)(2,1)S(1)}, bf16[32,1792]{1,0:T(8,128)(2,1)S(1)}, u32[]{:S(2)}, u32[]{:S(2)}) collective-permute-start(bf16[32,1792]{1,0:T(8,128)(2,1)S(1)} %get-tuple-element.21), channel_id=1, source_target_pairs={{0,16},{4,20},{8,24},{12,28},{16,32},{20,36},{24,40},{28,44},{32,4... | collective-permute-start | bytes 344072 | tf_op jit(solution)/shard_map/ppermute | solution.py:55
  74.9 6.7 %collective-permute-start.5 = (bf16[32,1792]{1,0:T(8,128)(2,1)S(1)}, bf16[32,1792]{1,0:T(8,128)(2,1)S(1)}, u32[]{:S(2)}, u32[]{:S(2)}) collective-permute-start(bf16[32,1792]{1,0:T(8,128)(2,1)S(1)} %get-tuple-element.22), channel_id=1, source_target_pairs={{0,52},{4,56},{8,60},{12,0},{16,4},{20,8},{24,12},{28,16},{32,20},... | collective-permute-start | bytes 344072 | tf_op jit(solution)/shard_map/ppermute | solution.py:55
  81.7 1.3 %collective-permute-done.4 = bf16[32,1792]{1,0:T(8,128)(2,1)S(1)} collective-permute-done((bf16[32,1792]{1,0:T(8,128)(2,1)S(1)}, bf16[32,1792]{1,0:T(8,128)(2,1)S(1)}, u32[]{:S(2)}, u32[]{:S(2)}) %collective-permute-start.4) | collective-permute-done | bytes 114720 | tf_op jit(solution)/shard_map/ppermute | solution.py:55
  83.0 5.1 %collective-permute-done.5 = bf16[32,1792]{1,0:T(8,128)(2,1)S(1)} collective-permute-done((bf16[32,1792]{1,0:T(8,128)(2,1)S(1)}, bf16[32,1792]{1,0:T(8,128)(2,1)S(1)}, u32[]{:S(2)}, u32[]{:S(2)}) %collective-permute-start.5) | collective-permute-done | bytes 114720 | tf_op jit(solution)/shard_map/ppermute | solution.py:55
  88.1 0.1 fusion.11
  88.2 8.5 %all_to_all.10 = bf16[4,8,1792]{2,1,0:T(8,128)(2,1)S(1)} all-to-all(bf16[4,8,1792]{2,1,0:T(8,128)(2,1)S(1)} %fusion.11), channel_id=1, replica_groups=mesh['mp'=16,'intra'=16,'inter'=4] {'inter'}, dimensions={0} | all-to-all | bytes 229376 | tf_op jit(solution)/shard_map/all_to_all | solution.py:92
  96.7 0.6 convert_reduce_fusion
  (13 shorter events, 0.2 us)
Async XLA Ops:
  0.0 23.6 %copy-start = (bf16[512,1792]{1,0:T(8,128)(2,1)S(1)}, bf16[512,1792]{1,0:T(8,128)(2,1)}, u32[]{:S(2)}) copy-start(bf16[512,1792]{1,0:T(8,128)(2,1)} %param.3) | copy-start | bytes 5505028
  9.9 11.0 %all-to-all-start = ((bf16[4,2,32,512]{3,2,1,0:T(8,128)(2,1)}), bf16[4,2,32,512]{3,2,1,0:T(8,128)(2,1)S(1)}, u32[]{:S(2)}, u32[]{:S(2)}) async-start(bf16[4,2,32,512]{3,2,1,0:T(8,128)(2,1)} %broadcast_in_dim.2), calls=%async_computation | async-start | bytes 524288 | tf_op jit(solution)/shard_map/all_to_all | solution.py:34
  24.6 28.0 %collective-permute-start = (bf16[160,1792]{1,0:T(8,128)(2,1)S(1)}, bf16[160,1792]{1,0:T(8,128)(2,1)S(1)}, u32[]{:S(2)}, u32[]{:S(2)}) collective-permute-start(bf16[160,1792]{1,0:T(8,128)(2,1)S(1)} %convolution_convert_fusion.2), channel_id=1, source_target_pairs={{0,4},{4,8},{8,12},{12,16},{16,20},{20,24},{24,28},{28,32},{32,36}... | collective-permute-start | bytes 1720328 | tf_op jit(solution)/shard_map/ppermute | solution.py:55
  28.9 26.5 %collective-permute-start.1 = (bf16[160,1792]{1,0:T(8,128)(2,1)S(1)}, bf16[160,1792]{1,0:T(8,128)(2,1)S(1)}, u32[]{:S(2)}, u32[]{:S(2)}) collective-permute-start(bf16[160,1792]{1,0:T(8,128)(2,1)S(1)} %convolution_convert_fusion.1), channel_id=1, source_target_pairs={{0,60},{4,0},{8,4},{12,8},{16,12},{20,16},{24,20},{28,24},{32,28},... | collective-permute-start | bytes 1720328 | tf_op jit(solution)/shard_map/ppermute | solution.py:55
  55.6 16.5 %collective-permute-start.2 = (bf16[64,1792]{1,0:T(8,128)(2,1)S(1)}, bf16[64,1792]{1,0:T(8,128)(2,1)S(1)}, u32[]{:S(2)}, u32[]{:S(2)}) collective-permute-start(bf16[64,1792]{1,0:T(8,128)(2,1)S(1)} %pad_maximum_fusion), channel_id=1, source_target_pairs={{0,12},{4,16},{8,20},{12,24},{16,28},{20,32},{24,36},{28,40},{32,4... | collective-permute-start | bytes 688136 | tf_op jit(solution)/shard_map/ppermute | solution.py:55
  57.5 11.5 %collective-permute-start.3 = (bf16[32,1792]{1,0:T(8,128)(2,1)S(1)}, bf16[32,1792]{1,0:T(8,128)(2,1)S(1)}, u32[]{:S(2)}, u32[]{:S(2)}) collective-permute-start(bf16[32,1792]{1,0:T(8,128)(2,1)S(1)} %get-tuple-element.18), channel_id=1, source_target_pairs={{0,52},{4,56},{8,60},{12,0},{16,4},{20,8},{24,12},{28,16},{32,20},... | collective-permute-start | bytes 344072 | tf_op jit(solution)/shard_map/ppermute | solution.py:55
  72.2 10.8 %collective-permute-start.4 = (bf16[32,1792]{1,0:T(8,128)(2,1)S(1)}, bf16[32,1792]{1,0:T(8,128)(2,1)S(1)}, u32[]{:S(2)}, u32[]{:S(2)}) collective-permute-start(bf16[32,1792]{1,0:T(8,128)(2,1)S(1)} %get-tuple-element.21), channel_id=1, source_target_pairs={{0,16},{4,20},{8,24},{12,28},{16,32},{20,36},{24,40},{28,44},{32,4... | collective-permute-start | bytes 344072 | tf_op jit(solution)/shard_map/ppermute | solution.py:55
  74.9 13.1 %collective-permute-start.5 = (bf16[32,1792]{1,0:T(8,128)(2,1)S(1)}, bf16[32,1792]{1,0:T(8,128)(2,1)S(1)}, u32[]{:S(2)}, u32[]{:S(2)}) collective-permute-start(bf16[32,1792]{1,0:T(8,128)(2,1)S(1)} %get-tuple-element.22), channel_id=1, source_target_pairs={{0,52},{4,56},{8,60},{12,0},{16,4},{20,8},{24,12},{28,16},{32,20},... | collective-permute-start | bytes 344072 | tf_op jit(solution)/shard_map/ppermute | solution.py:55

commit v7 on v6

--- a/solution.py
+++ b/solution.py
@@ -39,11 +39,10 @@
 
 
 ROUNDS = (
-    ((1, (1, 5, 8, -2, -5)), (-1, (-1, 2, 6, -4, -7))),
-    ((3, (3, 7)), (-3, (-6,))),
-    ((4, (4,)), (-3, (-3,))),
+    ((3, (8,)), (2, (2, 7, -3)), (-2, (-2, 3, -7)), (1, (1, 6, -4)), (-1, (-1, 4, -6))),
+    ((5, (5,)), (-5, (-5,))),
 )
-KEPT = (0, 3, 4, 7, -3, -6)
+KEPT = (0, 5, -5)
 
 
 def moved(block, step):

time: 99.2 us -> 104 us (1.048); the launches traced: 97.3 us -> 104 us
  blocking collectives: 19.8 us -> 24.8 us
  starting transfers between devices: 42.8 us -> 45.3 us
  waiting for transfers between devices: 30.7 us -> 29 us
  matrix products: 1.46 us -> 2.57 us
    all_to_all x1, blocking collectives: 8.5 us -> 13.4 us  [reduced(): lax.all_to_all(second, 'inter', split_axis=0, concat_axis=0, tiled=True)]
    ppermute x6 -> x7, starting transfers between devices: 38.5 us -> 41 us  [moved(): return lax.ppermute(block, ('mp', 'intra'), perm)]
    ppermute x6 -> x7, waiting for transfers between devices: 24 us -> 22.3 us  [moved(): return lax.ppermute(block, ('mp', 'intra'), perm)]
    dot_general x3 -> x6, matrix products: 1.46 us -> 2.57 us  [product(): lax.dot_general(rows, columns, (((1,), (0,)), ((), ())), preferred_elemen...]
  transfers between devices with their start and end apart: 7 -> 8, of which waited for: 7 -> 3; matrix products, arithmetic and copies ran while one was open for 1% -> 2% of each run, Pallas kernels for 0% -> 0%
where the time goes in v7:
time: 104 us
  starting transfers between devices  45.3 us (44%)
  waiting for transfers between devices  29 us (28%)
  blocking collectives  24.8 us (24%)
  matrix products  2.57 us (2%)
  other arithmetic  1.33 us (1%)
    ppermute x7, starting transfers between devices, moved(): return lax.ppermute(block, ('mp', 'intra'), perm)  41 us
    ppermute x7, waiting for transfers between devices, moved(): return lax.ppermute(block, ('mp', 'intra'), perm)  22.3 us
    all_to_all x1, blocking collectives, reduced(): lax.all_to_all(second, 'inter', split_axis=0, concat_axis=0, tiled=True)  13.4 us
    all_gather x1, blocking collectives, gathered(): out = lax.all_gather(own, 'mp', axis_index_groups=far)  9.18 us
    all_to_all x1, waiting for transfers between devices, gathered(): lax.all_to_all(out, 'mp', split_axis=0, concat_axis=0, tiled=True, axis_i...  6.68 us
    all_to_all x1, starting transfers between devices, gathered(): lax.all_to_all(out, 'mp', split_axis=0, concat_axis=0, tiled=True, axis_i...  4.29 us
    dot_general x6, matrix products, product(): lax.dot_general(rows, columns, (((1,), (0,)), ((), ())), preferred_elemen...  2.57 us
    all_gather x1, blocking collectives, gathered(): out = lax.all_gather(out, 'mp', axis_index_groups=pair)  2.17 us
  transfers between devices with their start and end apart: 8, of which 3 were waited for; matrix products, arithmetic and copies ran while one was open for 2% of the time, Pallas kernels for 0%

profile of v7, /device:TPU:56, one launch (start us, length us, event | category | flops | bytes accessed | tf_op | source)
XLA Modules:
  0.0 104.0 jit_solution(8921019078074985319)
XLA Ops:
  0.0 0.0 copy-start
  0.0 9.2 %all-gather = bf16[64,512]{1,0:T(8,128)(2,1)S(1)} all-gather(bf16[32,512]{1,0:T(8,128)(2,1)} %bitcast.52), channel_id=2, replica_groups={{0,512},{64,576},{128,640},{192,704},{256,768},{320,832},{384,896},{448..., dimensions={0}, use_global_device_ids=true | all-gather | bytes 98304 | tf_op jit(solution)/shard_map/all_gather | solution.py:32
  9.2 0.7 broadcast_in_dim.2
  9.9 4.3 %all-to-all-start = ((bf16[4,2,32,512]{3,2,1,0:T(8,128)(2,1)}), bf16[4,2,32,512]{3,2,1,0:T(8,128)(2,1)S(1)}, u32[]{:S(2)}, u32[]{:S(2)}) async-start(bf16[4,2,32,512]{3,2,1,0:T(8,128)(2,1)} %broadcast_in_dim.2), calls=%async_computation | async-start | bytes 524288 | tf_op jit(solution)/shard_map/all_to_all | solution.py:34
  14.2 6.7 %all-to-all-done = bf16[4,2,32,512]{3,2,1,0:T(8,128)(2,1)S(1)} async-done(((bf16[4,2,32,512]{3,2,1,0:T(8,128)(2,1)}), bf16[4,2,32,512]{3,2,1,0:T(8,128)(2,1)S(1)}, u32[]{:S(2)}, u32[]{:S(2)}) %all-to-all-start) | async-done | bytes 262176 | tf_op jit(solution)/shard_map/all_to_all | solution.py:34
  20.9 2.2 %all-gather.1 = bf16[8,2,32,512]{3,2,1,0:T(8,128)(2,1)S(1)} all-gather(bf16[4,2,32,512]{3,2,1,0:T(8,128)(2,1)S(1)} %all-to-all-done), channel_id=3, replica_groups={{0,64},{128,192},{256,320},{384,448},{512,576},{640,704},{768,832},{896..., dimensions={0}, use_global_device_ids=true | all-gather | bytes 786432 | tf_op jit(solution)/shard_map/all_gather | solution.py:37
  23.2 0.1 maximum_select_fusion
  23.3 0.2 fusion.1
  23.6 0.4 convolution_convert_fusion.3
  24.0 6.1 %collective-permute-start.1 = (bf16[96,1792]{1,0:T(8,128)(2,1)S(1)}, bf16[96,1792]{1,0:T(8,128)(2,1)S(1)}, u32[]{:S(2)}, u32[]{:S(2)}) collective-permute-start(bf16[96,1792]{1,0:T(8,128)(2,1)S(1)} %convolution_convert_fusion.3), channel_id=1, source_target_pairs={{0,8},{4,12},{8,16},{12,20},{16,24},{20,28},{24,32},{28,36},{32,40... | collective-permute-start | bytes 1032200 | tf_op jit(solution)/shard_map/ppermute | solution.py:54
  30.1 0.4 convolution_convert_fusion.2
  30.5 14.0 %collective-permute-start.2 = (bf16[96,1792]{1,0:T(8,128)(2,1)S(1)}, bf16[96,1792]{1,0:T(8,128)(2,1)S(1)}, u32[]{:S(2)}, u32[]{:S(2)}) collective-permute-start(bf16[96,1792]{1,0:T(8,128)(2,1)S(1)} %convolution_convert_fusion.2), channel_id=1, source_target_pairs={{0,56},{4,60},{8,0},{12,4},{16,8},{20,12},{24,16},{28,20},{32,24},... | collective-permute-start | bytes 1032200 | tf_op jit(solution)/shard_map/ppermute | solution.py:54
  44.6 0.4 convolution_convert_fusion.1
  45.0 3.4 %collective-permute-start.3 = (bf16[96,1792]{1,0:T(8,128)(2,1)S(1)}, bf16[96,1792]{1,0:T(8,128)(2,1)S(1)}, u32[]{:S(2)}, u32[]{:S(2)}) collective-permute-start(bf16[96,1792]{1,0:T(8,128)(2,1)S(1)} %convolution_convert_fusion.1), channel_id=1, source_target_pairs={{0,4},{4,8},{8,12},{12,16},{16,20},{20,24},{24,28},{28,32},{32,36}... | collective-permute-start | bytes 1032200 | tf_op jit(solution)/shard_map/ppermute | solution.py:54
  48.4 0.4 convolution_convert_fusion
  48.9 3.7 %collective-permute-start.4 = (bf16[96,1792]{1,0:T(8,128)(2,1)S(1)}, bf16[96,1792]{1,0:T(8,128)(2,1)S(1)}, u32[]{:S(2)}, u32[]{:S(2)}) collective-permute-start(bf16[96,1792]{1,0:T(8,128)(2,1)S(1)} %convolution_convert_fusion), channel_id=1, source_target_pairs={{0,60},{4,0},{8,4},{12,8},{16,12},{20,16},{24,20},{28,24},{32,28},... | collective-permute-start | bytes 1032200 | tf_op jit(solution)/shard_map/ppermute | solution.py:54
  52.5 0.4 convolution_convert_fusion.5
  52.9 1.9 %collective-permute-start = (bf16[32,1792]{1,0:T(8,128)(2,1)S(1)}, bf16[32,1792]{1,0:T(8,128)(2,1)S(1)}, u32[]{:S(2)}, u32[]{:S(2)}) collective-permute-start(bf16[32,1792]{1,0:T(8,128)(2,1)S(1)} %convolution_convert_fusion.5), channel_id=1, source_target_pairs={{0,12},{4,16},{8,20},{12,24},{16,28},{20,32},{24,36},{28,40},{32,4... | collective-permute-start | bytes 344072 | tf_op jit(solution)/shard_map/ppermute | solution.py:54
  54.9 0.4 fusion
  55.3 16.3 %collective-permute-done = bf16[32,1792]{1,0:T(8,128)(2,1)S(1)} collective-permute-done((bf16[32,1792]{1,0:T(8,128)(2,1)S(1)}, bf16[32,1792]{1,0:T(8,128)(2,1)S(1)}, u32[]{:S(2)}, u32[]{:S(2)}) %collective-permute-start) | collective-permute-done | bytes 114720 | tf_op jit(solution)/shard_map/ppermute | solution.py:54
  71.6 0.0 collective-permute-done.1
  71.6 0.0 collective-permute-done.2
  71.6 0.0 collective-permute-done.3
  71.6 0.0 collective-permute-done.4
  71.8 0.1 fusion.2
  71.9 1.9 %collective-permute-start.5 = (bf16[32,1792]{1,0:T(8,128)(2,1)S(1)}, bf16[32,1792]{1,0:T(8,128)(2,1)S(1)}, u32[]{:S(2)}, u32[]{:S(2)}) collective-permute-start(bf16[32,1792]{1,0:T(8,128)(2,1)S(1)} %get-tuple-element.19), channel_id=1, source_target_pairs={{0,20},{4,24},{8,28},{12,32},{16,36},{20,40},{24,44},{28,48},{32,5... | collective-permute-start | bytes 344072 | tf_op jit(solution)/shard_map/ppermute | solution.py:54
  73.9 9.9 %collective-permute-start.6 = (bf16[32,1792]{1,0:T(8,128)(2,1)S(1)}, bf16[32,1792]{1,0:T(8,128)(2,1)S(1)}, u32[]{:S(2)}, u32[]{:S(2)}) collective-permute-start(bf16[32,1792]{1,0:T(8,128)(2,1)S(1)} %get-tuple-element.20), channel_id=1, source_target_pairs={{0,44},{4,48},{8,52},{12,56},{16,60},{20,0},{24,4},{28,8},{32,12},... | collective-permute-start | bytes 344072 | tf_op jit(solution)/shard_map/ppermute | solution.py:54
  83.8 6.1 %collective-permute-done.5 = bf16[32,1792]{1,0:T(8,128)(2,1)S(1)} collective-permute-done((bf16[32,1792]{1,0:T(8,128)(2,1)S(1)}, bf16[32,1792]{1,0:T(8,128)(2,1)S(1)}, u32[]{:S(2)}, u32[]{:S(2)}) %collective-permute-start.5) | collective-permute-done | bytes 114720 | tf_op jit(solution)/shard_map/ppermute | solution.py:54
  89.9 0.0 collective-permute-done.6
  89.9 0.1 fusion.7
  89.9 13.4 %all_to_all.10 = bf16[4,8,1792]{2,1,0:T(8,128)(2,1)S(1)} all-to-all(bf16[4,8,1792]{2,1,0:T(8,128)(2,1)S(1)} %fusion.7), channel_id=1, replica_groups=mesh['mp'=16,'intra'=16,'inter'=4] {'inter'}, dimensions={0} | all-to-all | bytes 229376 | tf_op jit(solution)/shard_map/all_to_all | solution.py:91
  103.4 0.6 convert_reduce_fusion
  (10 shorter events, 0.3 us)
Async XLA Ops:
  0.0 23.6 %copy-start = (bf16[512,1792]{1,0:T(8,128)(2,1)S(1)}, bf16[512,1792]{1,0:T(8,128)(2,1)}, u32[]{:S(2)}) copy-start(bf16[512,1792]{1,0:T(8,128)(2,1)} %param.3) | copy-start | bytes 5505028
  9.9 11.0 %all-to-all-start = ((bf16[4,2,32,512]{3,2,1,0:T(8,128)(2,1)}), bf16[4,2,32,512]{3,2,1,0:T(8,128)(2,1)S(1)}, u32[]{:S(2)}, u32[]{:S(2)}) async-start(bf16[4,2,32,512]{3,2,1,0:T(8,128)(2,1)} %broadcast_in_dim.2), calls=%async_computation | async-start | bytes 524288 | tf_op jit(solution)/shard_map/all_to_all | solution.py:34
  24.0 47.6 %collective-permute-start.1 = (bf16[96,1792]{1,0:T(8,128)(2,1)S(1)}, bf16[96,1792]{1,0:T(8,128)(2,1)S(1)}, u32[]{:S(2)}, u32[]{:S(2)}) collective-permute-start(bf16[96,1792]{1,0:T(8,128)(2,1)S(1)} %convolution_convert_fusion.3), channel_id=1, source_target_pairs={{0,8},{4,12},{8,16},{12,20},{16,24},{20,28},{24,32},{28,36},{32,40... | collective-permute-start | bytes 1032200 | tf_op jit(solution)/shard_map/ppermute | solution.py:54
  30.5 41.0 %collective-permute-start.2 = (bf16[96,1792]{1,0:T(8,128)(2,1)S(1)}, bf16[96,1792]{1,0:T(8,128)(2,1)S(1)}, u32[]{:S(2)}, u32[]{:S(2)}) collective-permute-start(bf16[96,1792]{1,0:T(8,128)(2,1)S(1)} %convolution_convert_fusion.2), channel_id=1, source_target_pairs={{0,56},{4,60},{8,0},{12,4},{16,8},{20,12},{24,16},{28,20},{32,24},... | collective-permute-start | bytes 1032200 | tf_op jit(solution)/shard_map/ppermute | solution.py:54
  45.0 26.6 %collective-permute-start.3 = (bf16[96,1792]{1,0:T(8,128)(2,1)S(1)}, bf16[96,1792]{1,0:T(8,128)(2,1)S(1)}, u32[]{:S(2)}, u32[]{:S(2)}) collective-permute-start(bf16[96,1792]{1,0:T(8,128)(2,1)S(1)} %convolution_convert_fusion.1), channel_id=1, source_target_pairs={{0,4},{4,8},{8,12},{12,16},{16,20},{20,24},{24,28},{28,32},{32,36}... | collective-permute-start | bytes 1032200 | tf_op jit(solution)/shard_map/ppermute | solution.py:54
  48.9 22.7 %collective-permute-start.4 = (bf16[96,1792]{1,0:T(8,128)(2,1)S(1)}, bf16[96,1792]{1,0:T(8,128)(2,1)S(1)}, u32[]{:S(2)}, u32[]{:S(2)}) collective-permute-start(bf16[96,1792]{1,0:T(8,128)(2,1)S(1)} %convolution_convert_fusion), channel_id=1, source_target_pairs={{0,60},{4,0},{8,4},{12,8},{16,12},{20,16},{24,20},{28,24},{32,28},... | collective-permute-start | bytes 1032200 | tf_op jit(solution)/shard_map/ppermute | solution.py:54
  52.9 18.6 %collective-permute-start = (bf16[32,1792]{1,0:T(8,128)(2,1)S(1)}, bf16[32,1792]{1,0:T(8,128)(2,1)S(1)}, u32[]{:S(2)}, u32[]{:S(2)}) collective-permute-start(bf16[32,1792]{1,0:T(8,128)(2,1)S(1)} %convolution_convert_fusion.5), channel_id=1, source_target_pairs={{0,12},{4,16},{8,20},{12,24},{16,28},{20,32},{24,36},{28,40},{32,4... | collective-permute-start | bytes 344072 | tf_op jit(solution)/shard_map/ppermute | solution.py:54
  71.9 17.9 %collective-permute-start.5 = (bf16[32,1792]{1,0:T(8,128)(2,1)S(1)}, bf16[32,1792]{1,0:T(8,128)(2,1)S(1)}, u32[]{:S(2)}, u32[]{:S(2)}) collective-permute-start(bf16[32,1792]{1,0:T(8,128)(2,1)S(1)} %get-tuple-element.19), channel_id=1, source_target_pairs={{0,20},{4,24},{8,28},{12,32},{16,36},{20,40},{24,44},{28,48},{32,5... | collective-permute-start | bytes 344072 | tf_op jit(solution)/shard_map/ppermute | solution.py:54
  73.9 16.0 %collective-permute-start.6 = (bf16[32,1792]{1,0:T(8,128)(2,1)S(1)}, bf16[32,1792]{1,0:T(8,128)(2,1)S(1)}, u32[]{:S(2)}, u32[]{:S(2)}) collective-permute-start(bf16[32,1792]{1,0:T(8,128)(2,1)S(1)} %get-tuple-element.20), channel_id=1, source_target_pairs={{0,44},{4,48},{8,52},{12,56},{16,60},{20,0},{24,4},{28,8},{32,12},... | collective-permute-start | bytes 344072 | tf_op jit(solution)/shard_map/ppermute | solution.py:54

commit v8 on v7

--- a/solution.py
+++ b/solution.py
@@ -39,10 +39,11 @@
 
 
 ROUNDS = (
-    ((3, (8,)), (2, (2, 7, -3)), (-2, (-2, 3, -7)), (1, (1, 6, -4)), (-1, (-1, 4, -6))),
-    ((5, (5,)), (-5, (-5,))),
+    ((1, (1, 4, 7, -2, -5)), (-1, (-1, 2, 5, -4, -7)), (2, (8,))),
+    ((3, (6,)), (-3, (-6,))),
+    ((3, (3,)), (-3, (-3,))),
 )
-KEPT = (0, 5, -5)
+KEPT = (0, 3, -3, 6, -6)
 
 
 def moved(block, step):

time: 104 us -> 99.6 us (0.958); the launches traced: 104 us -> 98.4 us
  blocking collectives: 24.8 us -> 20.4 us
    all_to_all x1, blocking collectives: 13.4 us -> 9 us  [reduced(): lax.all_to_all(second, 'inter', split_axis=0, concat_axis=0, tiled=True)]
    dot_general x6 -> x4, matrix products: 2.57 us -> 1.81 us  [product(): lax.dot_general(rows, columns, (((1,), (0,)), ((), ())), preferred_elemen...]
  transfers between devices with their start and end apart: 8 -> 8, of which waited for: 3 -> 6; matrix products, arithmetic and copies ran while one was open for 2% -> 1% of each run, Pallas kernels for 0% -> 0%
where the time goes in v8:
time: 99.6 us; the launch traced here: 98.4 us
  starting transfers between devices  44.5 us (45%)
  waiting for transfers between devices  29.3 us (29%)
  blocking collectives  20.4 us (20%)
  matrix products  1.81 us (2%)
  other arithmetic  1.31 us (1%)
    ppermute x7, starting transfers between devices, moved(): return lax.ppermute(block, ('mp', 'intra'), perm)  40.2 us
    ppermute x7, waiting for transfers between devices, moved(): return lax.ppermute(block, ('mp', 'intra'), perm)  22.6 us
    all_gather x1, blocking collectives, gathered(): out = lax.all_gather(own, 'mp', axis_index_groups=far)  9.18 us
    all_to_all x1, blocking collectives, reduced(): lax.all_to_all(second, 'inter', split_axis=0, concat_axis=0, tiled=True)  9 us
    all_to_all x1, waiting for transfers between devices, gathered(): lax.all_to_all(out, 'mp', split_axis=0, concat_axis=0, tiled=True, axis_i...  6.68 us
    all_to_all x1, starting transfers between devices, gathered(): lax.all_to_all(out, 'mp', split_axis=0, concat_axis=0, tiled=True, axis_i...  4.29 us
    all_gather x1, blocking collectives, gathered(): out = lax.all_gather(out, 'mp', axis_index_groups=pair)  2.17 us
  transfers between devices with their start and end apart: 8, of which 6 were waited for; matrix products, arithmetic and copies ran while one was open for 1% of the time, Pallas kernels for 0%

profile of v8, /device:TPU:56, one launch (start us, length us, event | category | flops | bytes accessed | tf_op | source)
XLA Modules:
  0.0 98.4 jit_solution(6786956015191727208)
XLA Ops:
  0.0 9.2 %all-gather = bf16[64,512]{1,0:T(8,128)(2,1)S(1)} all-gather(bf16[32,512]{1,0:T(8,128)(2,1)} %bitcast.83), channel_id=2, replica_groups={{0,512},{64,576},{128,640},{192,704},{256,768},{320,832},{384,896},{448..., dimensions={0}, use_global_device_ids=true | all-gather | bytes 98304 | tf_op jit(solution)/shard_map/all_gather | solution.py:32
  9.2 0.7 broadcast_in_dim.2
  9.9 4.3 %all-to-all-start = ((bf16[4,2,32,512]{3,2,1,0:T(8,128)(2,1)}), bf16[4,2,32,512]{3,2,1,0:T(8,128)(2,1)S(1)}, u32[]{:S(2)}, u32[]{:S(2)}) async-start(bf16[4,2,32,512]{3,2,1,0:T(8,128)(2,1)} %broadcast_in_dim.2), calls=%async_computation | async-start | bytes 524288 | tf_op jit(solution)/shard_map/all_to_all | solution.py:34
  14.2 6.7 %all-to-all-done = bf16[4,2,32,512]{3,2,1,0:T(8,128)(2,1)S(1)} async-done(((bf16[4,2,32,512]{3,2,1,0:T(8,128)(2,1)}), bf16[4,2,32,512]{3,2,1,0:T(8,128)(2,1)S(1)}, u32[]{:S(2)}, u32[]{:S(2)}) %all-to-all-start) | async-done | bytes 262176 | tf_op jit(solution)/shard_map/all_to_all | solution.py:34
  20.9 2.2 %all-gather.1 = bf16[8,2,32,512]{3,2,1,0:T(8,128)(2,1)S(1)} all-gather(bf16[4,2,32,512]{3,2,1,0:T(8,128)(2,1)S(1)} %all-to-all-done), channel_id=3, replica_groups={{0,64},{128,192},{256,320},{384,448},{512,576},{640,704},{768,832},{896..., dimensions={0}, use_global_device_ids=true | all-gather | bytes 786432 | tf_op jit(solution)/shard_map/all_gather | solution.py:37
  23.2 0.1 maximum_select_fusion
  23.3 0.2 fusion.1
  23.6 0.5 convolution_convert_fusion.1
  24.1 4.3 %collective-permute-start = (bf16[160,1792]{1,0:T(8,128)(2,1)S(1)}, bf16[160,1792]{1,0:T(8,128)(2,1)S(1)}, u32[]{:S(2)}, u32[]{:S(2)}) collective-permute-start(bf16[160,1792]{1,0:T(8,128)(2,1)S(1)} %convolution_convert_fusion.1), channel_id=1, source_target_pairs={{0,4},{4,8},{8,12},{12,16},{16,20},{20,24},{24,28},{28,32},{32,36}... | collective-permute-start | bytes 1720328 | tf_op jit(solution)/shard_map/ppermute | solution.py:55
  28.4 0.5 convolution_convert_fusion
  28.9 15.9 %collective-permute-start.1 = (bf16[160,1792]{1,0:T(8,128)(2,1)S(1)}, bf16[160,1792]{1,0:T(8,128)(2,1)S(1)}, u32[]{:S(2)}, u32[]{:S(2)}) collective-permute-start(bf16[160,1792]{1,0:T(8,128)(2,1)S(1)} %convolution_convert_fusion), channel_id=1, source_target_pairs={{0,60},{4,0},{8,4},{12,8},{16,12},{20,16},{24,20},{28,24},{32,28},... | collective-permute-start | bytes 1720328 | tf_op jit(solution)/shard_map/ppermute | solution.py:55
  44.7 0.4 convolution_convert_fusion.3
  45.1 1.9 %collective-permute-start.2 = (bf16[32,1792]{1,0:T(8,128)(2,1)S(1)}, bf16[32,1792]{1,0:T(8,128)(2,1)S(1)}, u32[]{:S(2)}, u32[]{:S(2)}) collective-permute-start(bf16[32,1792]{1,0:T(8,128)(2,1)S(1)} %convolution_convert_fusion.3), channel_id=1, source_target_pairs={{0,8},{4,12},{8,16},{12,20},{16,24},{20,28},{24,32},{28,36},{32,40... | collective-permute-start | bytes 344072 | tf_op jit(solution)/shard_map/ppermute | solution.py:55
  47.1 0.5 fusion
  47.5 11.8 %collective-permute-done.2 = bf16[32,1792]{1,0:T(8,128)(2,1)S(1)} collective-permute-done((bf16[32,1792]{1,0:T(8,128)(2,1)S(1)}, bf16[32,1792]{1,0:T(8,128)(2,1)S(1)}, u32[]{:S(2)}, u32[]{:S(2)}) %collective-permute-start.2) | collective-permute-done | bytes 114720 | tf_op jit(solution)/shard_map/ppermute | solution.py:55
  59.4 0.0 collective-permute-done
  59.4 0.0 collective-permute-done.1
  59.4 0.1 convert_element_type.66
  59.5 0.1 convert_element_type.67
  59.6 0.1 fusion.4
  59.6 1.9 %collective-permute-start.3 = (bf16[32,1792]{1,0:T(8,128)(2,1)S(1)}, bf16[32,1792]{1,0:T(8,128)(2,1)S(1)}, u32[]{:S(2)}, u32[]{:S(2)}) collective-permute-start(bf16[32,1792]{1,0:T(8,128)(2,1)S(1)} %get-tuple-element.19), channel_id=1, source_target_pairs={{0,12},{4,16},{8,20},{12,24},{16,28},{20,32},{24,36},{28,40},{32,4... | collective-permute-start | bytes 344072 | tf_op jit(solution)/shard_map/ppermute | solution.py:55
  61.6 6.9 %collective-permute-start.4 = (bf16[32,1792]{1,0:T(8,128)(2,1)S(1)}, bf16[32,1792]{1,0:T(8,128)(2,1)S(1)}, u32[]{:S(2)}, u32[]{:S(2)}) collective-permute-start(bf16[32,1792]{1,0:T(8,128)(2,1)S(1)} %get-tuple-element.20), channel_id=1, source_target_pairs={{0,52},{4,56},{8,60},{12,0},{16,4},{20,8},{24,12},{28,16},{32,20},... | collective-permute-start | bytes 344072 | tf_op jit(solution)/shard_map/ppermute | solution.py:55
  68.5 2.9 %collective-permute-done.3 = bf16[32,1792]{1,0:T(8,128)(2,1)S(1)} collective-permute-done((bf16[32,1792]{1,0:T(8,128)(2,1)S(1)}, bf16[32,1792]{1,0:T(8,128)(2,1)S(1)}, u32[]{:S(2)}, u32[]{:S(2)}) %collective-permute-start.3) | collective-permute-done | bytes 114720 | tf_op jit(solution)/shard_map/ppermute | solution.py:55
  71.4 0.8 collective-permute-done.4
  72.2 0.1 fusion.3
  72.3 2.0 %collective-permute-start.5 = (bf16[32,1792]{1,0:T(8,128)(2,1)S(1)}, bf16[32,1792]{1,0:T(8,128)(2,1)S(1)}, u32[]{:S(2)}, u32[]{:S(2)}) collective-permute-start(bf16[32,1792]{1,0:T(8,128)(2,1)S(1)} %get-tuple-element.23), channel_id=1, source_target_pairs={{0,12},{4,16},{8,20},{12,24},{16,28},{20,32},{24,36},{28,40},{32,4... | collective-permute-start | bytes 344072 | tf_op jit(solution)/shard_map/ppermute | solution.py:55
  74.2 7.4 %collective-permute-start.6 = (bf16[32,1792]{1,0:T(8,128)(2,1)S(1)}, bf16[32,1792]{1,0:T(8,128)(2,1)S(1)}, u32[]{:S(2)}, u32[]{:S(2)}) collective-permute-start(bf16[32,1792]{1,0:T(8,128)(2,1)S(1)} %get-tuple-element.24), channel_id=1, source_target_pairs={{0,52},{4,56},{8,60},{12,0},{16,4},{20,8},{24,12},{28,16},{32,20},... | collective-permute-start | bytes 344072 | tf_op jit(solution)/shard_map/ppermute | solution.py:55
  81.6 0.8 collective-permute-done.5
  82.4 6.3 %collective-permute-done.6 = bf16[32,1792]{1,0:T(8,128)(2,1)S(1)} collective-permute-done((bf16[32,1792]{1,0:T(8,128)(2,1)S(1)}, bf16[32,1792]{1,0:T(8,128)(2,1)S(1)}, u32[]{:S(2)}, u32[]{:S(2)}) %collective-permute-start.6) | collective-permute-done | bytes 114720 | tf_op jit(solution)/shard_map/ppermute | solution.py:55
  88.7 0.1 fusion.12
  88.8 9.0 %all_to_all.10 = bf16[4,8,1792]{2,1,0:T(8,128)(2,1)S(1)} all-to-all(bf16[4,8,1792]{2,1,0:T(8,128)(2,1)S(1)} %fusion.12), channel_id=1, replica_groups=mesh['mp'=16,'intra'=16,'inter'=4] {'inter'}, dimensions={0} | all-to-all | bytes 229376 | tf_op jit(solution)/shard_map/all_to_all | solution.py:92
  97.8 0.6 convert_reduce_fusion
  (11 shorter events, 0.2 us)
Async XLA Ops:
  0.0 23.6 %copy-start = (bf16[512,1792]{1,0:T(8,128)(2,1)S(1)}, bf16[512,1792]{1,0:T(8,128)(2,1)}, u32[]{:S(2)}) copy-start(bf16[512,1792]{1,0:T(8,128)(2,1)} %param.3) | copy-start | bytes 5505028
  9.9 11.0 %all-to-all-start = ((bf16[4,2,32,512]{3,2,1,0:T(8,128)(2,1)}), bf16[4,2,32,512]{3,2,1,0:T(8,128)(2,1)S(1)}, u32[]{:S(2)}, u32[]{:S(2)}) async-start(bf16[4,2,32,512]{3,2,1,0:T(8,128)(2,1)} %broadcast_in_dim.2), calls=%async_computation | async-start | bytes 524288 | tf_op jit(solution)/shard_map/all_to_all | solution.py:34
  24.1 35.3 %collective-permute-start = (bf16[160,1792]{1,0:T(8,128)(2,1)S(1)}, bf16[160,1792]{1,0:T(8,128)(2,1)S(1)}, u32[]{:S(2)}, u32[]{:S(2)}) collective-permute-start(bf16[160,1792]{1,0:T(8,128)(2,1)S(1)} %convolution_convert_fusion.1), channel_id=1, source_target_pairs={{0,4},{4,8},{8,12},{12,16},{16,20},{20,24},{24,28},{28,32},{32,36}... | collective-permute-start | bytes 1720328 | tf_op jit(solution)/shard_map/ppermute | solution.py:55
  28.9 30.5 %collective-permute-start.1 = (bf16[160,1792]{1,0:T(8,128)(2,1)S(1)}, bf16[160,1792]{1,0:T(8,128)(2,1)S(1)}, u32[]{:S(2)}, u32[]{:S(2)}) collective-permute-start(bf16[160,1792]{1,0:T(8,128)(2,1)S(1)} %convolution_convert_fusion), channel_id=1, source_target_pairs={{0,60},{4,0},{8,4},{12,8},{16,12},{20,16},{24,20},{28,24},{32,28},... | collective-permute-start | bytes 1720328 | tf_op jit(solution)/shard_map/ppermute | solution.py:55
  45.1 14.2 %collective-permute-start.2 = (bf16[32,1792]{1,0:T(8,128)(2,1)S(1)}, bf16[32,1792]{1,0:T(8,128)(2,1)S(1)}, u32[]{:S(2)}, u32[]{:S(2)}) collective-permute-start(bf16[32,1792]{1,0:T(8,128)(2,1)S(1)} %convolution_convert_fusion.3), channel_id=1, source_target_pairs={{0,8},{4,12},{8,16},{12,20},{16,24},{20,28},{24,32},{28,36},{32,40... | collective-permute-start | bytes 344072 | tf_op jit(solution)/shard_map/ppermute | solution.py:55
  59.6 11.7 %collective-permute-start.3 = (bf16[32,1792]{1,0:T(8,128)(2,1)S(1)}, bf16[32,1792]{1,0:T(8,128)(2,1)S(1)}, u32[]{:S(2)}, u32[]{:S(2)}) collective-permute-start(bf16[32,1792]{1,0:T(8,128)(2,1)S(1)} %get-tuple-element.19), channel_id=1, source_target_pairs={{0,12},{4,16},{8,20},{12,24},{16,28},{20,32},{24,36},{28,40},{32,4... | collective-permute-start | bytes 344072 | tf_op jit(solution)/shard_map/ppermute | solution.py:55
  61.6 10.6 %collective-permute-start.4 = (bf16[32,1792]{1,0:T(8,128)(2,1)S(1)}, bf16[32,1792]{1,0:T(8,128)(2,1)S(1)}, u32[]{:S(2)}, u32[]{:S(2)}) collective-permute-start(bf16[32,1792]{1,0:T(8,128)(2,1)S(1)} %get-tuple-element.20), channel_id=1, source_target_pairs={{0,52},{4,56},{8,60},{12,0},{16,4},{20,8},{24,12},{28,16},{32,20},... | collective-permute-start | bytes 344072 | tf_op jit(solution)/shard_map/ppermute | solution.py:55
  72.3 10.2 %collective-permute-start.5 = (bf16[32,1792]{1,0:T(8,128)(2,1)S(1)}, bf16[32,1792]{1,0:T(8,128)(2,1)S(1)}, u32[]{:S(2)}, u32[]{:S(2)}) collective-permute-start(bf16[32,1792]{1,0:T(8,128)(2,1)S(1)} %get-tuple-element.23), channel_id=1, source_target_pairs={{0,12},{4,16},{8,20},{12,24},{16,28},{20,32},{24,36},{28,40},{32,4... | collective-permute-start | bytes 344072 | tf_op jit(solution)/shard_map/ppermute | solution.py:55
  74.2 14.5 %collective-permute-start.6 = (bf16[32,1792]{1,0:T(8,128)(2,1)S(1)}, bf16[32,1792]{1,0:T(8,128)(2,1)S(1)}, u32[]{:S(2)}, u32[]{:S(2)}) collective-permute-start(bf16[32,1792]{1,0:T(8,128)(2,1)S(1)} %get-tuple-element.24), channel_id=1, source_target_pairs={{0,52},{4,56},{8,60},{12,0},{16,4},{20,8},{24,12},{28,16},{32,20},... | collective-permute-start | bytes 344072 | tf_op jit(solution)/shard_map/ppermute | solution.py:55

commit v9 on v6

--- a/solution.py
+++ b/solution.py
@@ -55,9 +55,8 @@
     return lax.ppermute(block, ("mp", "intra"), perm)
 
 
-def reduced(features, cotangent):
+def reduced(features, cotangent, z, core):
     n, replicas = lax.axis_size("intra"), lax.axis_size("inter")
-    z, core = lax.axis_index("intra"), lax.axis_index("mp") % 2
     tokens = features.shape[1]
     cols = cotangent.shape[1]
     blocks = features.reshape(n, -1, tokens)
@@ -94,7 +93,10 @@
 
 
 def shards(activations, cotangent):
-    return reduced(gathered(activations), cotangent)
+    z, core = lax.axis_index("intra"), lax.axis_index("mp") % 2
+    activations, z, core = lax.optimization_barrier((activations, z, core))
+    features, z, core = lax.optimization_barrier((gathered(activations), z, core))
+    return reduced(features, cotangent, z, core)
 
 
 def solution(mesh):

time: 99.2 us -> 98.1 us (0.989)
  blocking collectives: 19.8 us -> 30.6 us
  waiting for transfers between devices: 30.7 us -> 24 us
  starting transfers between devices: 42.8 us -> 38.5 us
    all_to_all x0 -> x1, blocking collectives: none -> 10.8 us  [gathered(): lax.all_to_all(out, 'mp', split_axis=0, concat_axis=0, tiled=True, axis_i...]
    all_to_all x1 -> x0, waiting for transfers between devices: 6.68 us -> none  [gathered(): lax.all_to_all(out, 'mp', split_axis=0, concat_axis=0, tiled=True, axis_i...]
    all_to_all x1 -> x0, starting transfers between devices: 4.29 us -> none  [gathered(): lax.all_to_all(out, 'mp', split_axis=0, concat_axis=0, tiled=True, axis_i...]
  transfers between devices with their start and end apart: 7 -> 6, of which waited for: 7 -> 6; matrix products, arithmetic and copies ran while one was open for 1% -> 1% of each run, Pallas kernels for 0% -> 0%
where the time goes in v9:
time: 98.1 us; the launch traced here: 96.4 us
  starting transfers between devices  38.5 us (39%)
  blocking collectives  30.6 us (31%)
  waiting for transfers between devices  24 us (24%)
  matrix products  1.46 us (1%)
  other arithmetic  1.36 us (1%)
    ppermute x6, starting transfers between devices, moved(): return lax.ppermute(block, ('mp', 'intra'), perm)  38.5 us
    ppermute x6, waiting for transfers between devices, moved(): return lax.ppermute(block, ('mp', 'intra'), perm)  24 us
    all_to_all x1, blocking collectives, gathered(): lax.all_to_all(out, 'mp', split_axis=0, concat_axis=0, tiled=True, axis_i...  10.8 us
    all_gather x1, blocking collectives, gathered(): out = lax.all_gather(own, 'mp', axis_index_groups=far)  9.18 us
    all_to_all x1, blocking collectives, reduced(): lax.all_to_all(second, 'inter', split_axis=0, concat_axis=0, tiled=True)  8.46 us
    all_gather x1, blocking collectives, gathered(): out = lax.all_gather(out, 'mp', axis_index_groups=pair)  2.17 us
  transfers between devices with their start and end apart: 6, of which 6 were waited for; matrix products, arithmetic and copies ran while one was open for 1% of the time, Pallas kernels for 0%

profile of v9, /device:TPU:56, one launch (start us, length us, event | category | flops | bytes accessed | tf_op | source)
XLA Modules:
  0.0 96.4 jit_solution(8838024724812991050)
XLA Ops:
  0.0 0.0 copy-start
  0.0 9.2 %all-gather = bf16[64,512]{1,0:T(8,128)(2,1)S(1)} all-gather(bf16[32,512]{1,0:T(8,128)(2,1)} %bitcast.88), channel_id=2, replica_groups={{0,512},{64,576},{128,640},{192,704},{256,768},{320,832},{384,896},{448..., dimensions={0}, use_global_device_ids=true | all-gather | bytes 98304 | tf_op jit(solution)/shard_map/all_gather | solution.py:32
  9.2 10.8 %all_to_all.10 = bf16[4,2,32,512]{3,2,1,0:T(8,128)(2,1)S(1)} all-to-all(bf16[4,2,32,512]{3,2,1,0:T(8,128)(2,1)S(1)} %broadcast_in_dim.2), channel_id=1, replica_groups={{0,128,256,384},{64,192,320,448},{512,640,768,896},{576,704,832,960},{1..., dimensions={0} | all-to-all | bytes 524288 | tf_op jit(solution)/shard_map/all_to_all | solution.py:34
  20.0 2.2 %all-gather.1 = bf16[8,2,32,512]{3,2,1,0:T(8,128)(2,1)S(1)} all-gather(bf16[4,2,32,512]{3,2,1,0:T(8,128)(2,1)S(1)} %all_to_all.10), channel_id=3, replica_groups={{0,64},{128,192},{256,320},{384,448},{512,576},{640,704},{768,832},{896..., dimensions={0}, use_global_device_ids=true | all-gather | bytes 786432 | tf_op jit(solution)/shard_map/all_gather | solution.py:37
  22.3 0.1 maximum_select_fusion
  22.4 0.2 fusion.1
  22.7 0.0 copy-done
  22.7 0.5 convolution_convert_fusion.1
  23.2 0.5 convolution_convert_fusion.2
  23.7 4.3 %collective-permute-start = (bf16[160,1792]{1,0:T(8,128)(2,1)S(1)}, bf16[160,1792]{1,0:T(8,128)(2,1)S(1)}, u32[]{:S(2)}, u32[]{:S(2)}) collective-permute-start(bf16[160,1792]{1,0:T(8,128)(2,1)S(1)} %convolution_convert_fusion.2), channel_id=1, source_target_pairs={{0,4},{4,8},{8,12},{12,16},{16,20},{20,24},{24,28},{28,32},{32,36}... | collective-permute-start | bytes 1720328 | tf_op jit(solution)/shard_map/ppermute | solution.py:55
  28.0 15.9 %collective-permute-start.1 = (bf16[160,1792]{1,0:T(8,128)(2,1)S(1)}, bf16[160,1792]{1,0:T(8,128)(2,1)S(1)}, u32[]{:S(2)}, u32[]{:S(2)}) collective-permute-start(bf16[160,1792]{1,0:T(8,128)(2,1)S(1)} %convolution_convert_fusion.1), channel_id=1, source_target_pairs={{0,60},{4,0},{8,4},{12,8},{16,12},{20,16},{24,20},{28,24},{32,28},... | collective-permute-start | bytes 1720328 | tf_op jit(solution)/shard_map/ppermute | solution.py:55
  43.9 0.5 fusion
  44.4 7.3 %collective-permute-done = bf16[160,1792]{1,0:T(8,128)(2,1)S(1)} collective-permute-done((bf16[160,1792]{1,0:T(8,128)(2,1)S(1)}, bf16[160,1792]{1,0:T(8,128)(2,1)S(1)}, u32[]{:S(2)}, u32[]{:S(2)}) %collective-permute-start) | collective-permute-done | bytes 573472 | tf_op jit(solution)/shard_map/ppermute | solution.py:55
  51.6 2.8 %collective-permute-done.1 = bf16[160,1792]{1,0:T(8,128)(2,1)S(1)} collective-permute-done((bf16[160,1792]{1,0:T(8,128)(2,1)S(1)}, bf16[160,1792]{1,0:T(8,128)(2,1)S(1)}, u32[]{:S(2)}, u32[]{:S(2)}) %collective-permute-start.1) | collective-permute-done | bytes 573472 | tf_op jit(solution)/shard_map/ppermute | solution.py:55
  54.4 0.1 convert_element_type.61
  54.5 0.1 convert_element_type.62
  54.6 0.1 fusion.8
  54.7 1.9 %collective-permute-start.2 = (bf16[64,1792]{1,0:T(8,128)(2,1)S(1)}, bf16[64,1792]{1,0:T(8,128)(2,1)S(1)}, u32[]{:S(2)}, u32[]{:S(2)}) collective-permute-start(bf16[64,1792]{1,0:T(8,128)(2,1)S(1)} %pad_maximum_fusion), channel_id=1, source_target_pairs={{0,12},{4,16},{8,20},{12,24},{16,28},{20,32},{24,36},{28,40},{32,4... | collective-permute-start | bytes 688136 | tf_op jit(solution)/shard_map/ppermute | solution.py:55
  56.7 6.9 %collective-permute-start.3 = (bf16[32,1792]{1,0:T(8,128)(2,1)S(1)}, bf16[32,1792]{1,0:T(8,128)(2,1)S(1)}, u32[]{:S(2)}, u32[]{:S(2)}) collective-permute-start(bf16[32,1792]{1,0:T(8,128)(2,1)S(1)} %get-tuple-element.30), channel_id=1, source_target_pairs={{0,52},{4,56},{8,60},{12,0},{16,4},{20,8},{24,12},{28,16},{32,20},... | collective-permute-start | bytes 344072 | tf_op jit(solution)/shard_map/ppermute | solution.py:55
  63.6 4.6 %collective-permute-done.3 = bf16[32,1792]{1,0:T(8,128)(2,1)S(1)} collective-permute-done((bf16[32,1792]{1,0:T(8,128)(2,1)S(1)}, bf16[32,1792]{1,0:T(8,128)(2,1)S(1)}, u32[]{:S(2)}, u32[]{:S(2)}) %collective-permute-start.3) | collective-permute-done | bytes 114720 | tf_op jit(solution)/shard_map/ppermute | solution.py:55
  68.2 3.0 %collective-permute-done.2 = bf16[64,1792]{1,0:T(8,128)(2,1)S(1)} collective-permute-done((bf16[64,1792]{1,0:T(8,128)(2,1)S(1)}, bf16[64,1792]{1,0:T(8,128)(2,1)S(1)}, u32[]{:S(2)}, u32[]{:S(2)}) %collective-permute-start.2) | collective-permute-done | bytes 229408 | tf_op jit(solution)/shard_map/ppermute | solution.py:55
  71.2 0.1 fusion.3
  71.3 2.7 %collective-permute-start.4 = (bf16[32,1792]{1,0:T(8,128)(2,1)S(1)}, bf16[32,1792]{1,0:T(8,128)(2,1)S(1)}, u32[]{:S(2)}, u32[]{:S(2)}) collective-permute-start(bf16[32,1792]{1,0:T(8,128)(2,1)S(1)} %get-tuple-element.33), channel_id=1, source_target_pairs={{0,16},{4,20},{8,24},{12,28},{16,32},{20,36},{24,40},{28,44},{32,4... | collective-permute-start | bytes 344072 | tf_op jit(solution)/shard_map/ppermute | solution.py:55
  74.0 6.8 %collective-permute-start.5 = (bf16[32,1792]{1,0:T(8,128)(2,1)S(1)}, bf16[32,1792]{1,0:T(8,128)(2,1)S(1)}, u32[]{:S(2)}, u32[]{:S(2)}) collective-permute-start(bf16[32,1792]{1,0:T(8,128)(2,1)S(1)} %get-tuple-element.34), channel_id=1, source_target_pairs={{0,52},{4,56},{8,60},{12,0},{16,4},{20,8},{24,12},{28,16},{32,20},... | collective-permute-start | bytes 344072 | tf_op jit(solution)/shard_map/ppermute | solution.py:55
  80.8 1.3 %collective-permute-done.4 = bf16[32,1792]{1,0:T(8,128)(2,1)S(1)} collective-permute-done((bf16[32,1792]{1,0:T(8,128)(2,1)S(1)}, bf16[32,1792]{1,0:T(8,128)(2,1)S(1)}, u32[]{:S(2)}, u32[]{:S(2)}) %collective-permute-start.4) | collective-permute-done | bytes 114720 | tf_op jit(solution)/shard_map/ppermute | solution.py:55
  82.1 5.1 %collective-permute-done.5 = bf16[32,1792]{1,0:T(8,128)(2,1)S(1)} collective-permute-done((bf16[32,1792]{1,0:T(8,128)(2,1)S(1)}, bf16[32,1792]{1,0:T(8,128)(2,1)S(1)}, u32[]{:S(2)}, u32[]{:S(2)}) %collective-permute-start.5) | collective-permute-done | bytes 114720 | tf_op jit(solution)/shard_map/ppermute | solution.py:55
  87.2 0.1 fusion.11
  87.3 8.5 %all_to_all.11 = bf16[4,8,1792]{2,1,0:T(8,128)(2,1)S(1)} all-to-all(bf16[4,8,1792]{2,1,0:T(8,128)(2,1)S(1)} %fusion.11), channel_id=1, replica_groups=mesh['mp'=16,'intra'=16,'inter'=4] {'inter'}, dimensions={0} | all-to-all | bytes 229376 | tf_op jit(solution)/shard_map/all_to_all | solution.py:91
  95.7 0.6 convert_reduce_fusion
  (14 shorter events, 0.2 us)
Async XLA Ops:
  0.0 22.7 %copy-start = (bf16[512,1792]{1,0:T(8,128)(2,1)S(1)}, bf16[512,1792]{1,0:T(8,128)(2,1)}, u32[]{:S(2)}) copy-start(bf16[512,1792]{1,0:T(8,128)(2,1)} %param.3) | copy-start | bytes 5505028
  23.7 27.9 %collective-permute-start = (bf16[160,1792]{1,0:T(8,128)(2,1)S(1)}, bf16[160,1792]{1,0:T(8,128)(2,1)S(1)}, u32[]{:S(2)}, u32[]{:S(2)}) collective-permute-start(bf16[160,1792]{1,0:T(8,128)(2,1)S(1)} %convolution_convert_fusion.2), channel_id=1, source_target_pairs={{0,4},{4,8},{8,12},{12,16},{16,20},{20,24},{24,28},{28,32},{32,36}... | collective-permute-start | bytes 1720328 | tf_op jit(solution)/shard_map/ppermute | solution.py:55
  28.0 26.5 %collective-permute-start.1 = (bf16[160,1792]{1,0:T(8,128)(2,1)S(1)}, bf16[160,1792]{1,0:T(8,128)(2,1)S(1)}, u32[]{:S(2)}, u32[]{:S(2)}) collective-permute-start(bf16[160,1792]{1,0:T(8,128)(2,1)S(1)} %convolution_convert_fusion.1), channel_id=1, source_target_pairs={{0,60},{4,0},{8,4},{12,8},{16,12},{20,16},{24,20},{28,24},{32,28},... | collective-permute-start | bytes 1720328 | tf_op jit(solution)/shard_map/ppermute | solution.py:55
  54.7 16.5 %collective-permute-start.2 = (bf16[64,1792]{1,0:T(8,128)(2,1)S(1)}, bf16[64,1792]{1,0:T(8,128)(2,1)S(1)}, u32[]{:S(2)}, u32[]{:S(2)}) collective-permute-start(bf16[64,1792]{1,0:T(8,128)(2,1)S(1)} %pad_maximum_fusion), channel_id=1, source_target_pairs={{0,12},{4,16},{8,20},{12,24},{16,28},{20,32},{24,36},{28,40},{32,4... | collective-permute-start | bytes 688136 | tf_op jit(solution)/shard_map/ppermute | solution.py:55
  56.7 11.5 %collective-permute-start.3 = (bf16[32,1792]{1,0:T(8,128)(2,1)S(1)}, bf16[32,1792]{1,0:T(8,128)(2,1)S(1)}, u32[]{:S(2)}, u32[]{:S(2)}) collective-permute-start(bf16[32,1792]{1,0:T(8,128)(2,1)S(1)} %get-tuple-element.30), channel_id=1, source_target_pairs={{0,52},{4,56},{8,60},{12,0},{16,4},{20,8},{24,12},{28,16},{32,20},... | collective-permute-start | bytes 344072 | tf_op jit(solution)/shard_map/ppermute | solution.py:55
  71.3 10.8 %collective-permute-start.4 = (bf16[32,1792]{1,0:T(8,128)(2,1)S(1)}, bf16[32,1792]{1,0:T(8,128)(2,1)S(1)}, u32[]{:S(2)}, u32[]{:S(2)}) collective-permute-start(bf16[32,1792]{1,0:T(8,128)(2,1)S(1)} %get-tuple-element.33), channel_id=1, source_target_pairs={{0,16},{4,20},{8,24},{12,28},{16,32},{20,36},{24,40},{28,44},{32,4... | collective-permute-start | bytes 344072 | tf_op jit(solution)/shard_map/ppermute | solution.py:55
  74.0 13.2 %collective-permute-start.5 = (bf16[32,1792]{1,0:T(8,128)(2,1)S(1)}, bf16[32,1792]{1,0:T(8,128)(2,1)S(1)}, u32[]{:S(2)}, u32[]{:S(2)}) collective-permute-start(bf16[32,1792]{1,0:T(8,128)(2,1)S(1)} %get-tuple-element.34), channel_id=1, source_target_pairs={{0,52},{4,56},{8,60},{12,0},{16,4},{20,8},{24,12},{28,16},{32,20},... | collective-permute-start | bytes 344072 | tf_op jit(solution)/shard_map/ppermute | solution.py:55

commit v10 on v5

--- a/solution.py
+++ b/solution.py
@@ -52,9 +52,8 @@
     return lax.ppermute(block, ("mp", "intra"), perm)
 
 
-def reduced(features, cotangent):
+def reduced(features, cotangent, z, core):
     n, replicas = lax.axis_size("intra"), lax.axis_size("inter")
-    z, core = lax.axis_index("intra"), lax.axis_index("mp") % 2
     tokens = features.shape[1]
     cols = cotangent.shape[1]
     blocks = features.reshape(n, -1, tokens)
@@ -91,7 +90,10 @@
 
 
 def shards(activations, cotangent):
-    return reduced(gathered(activations), cotangent)
+    z, core = lax.axis_index("intra"), lax.axis_index("mp") % 2
+    activations, z, core = lax.optimization_barrier((activations, z, core))
+    features, z, core = lax.optimization_barrier((gathered(activations), z, core))
+    return reduced(features, cotangent, z, core)
 
 
 def solution(mesh):

time: 101 us -> 99.9 us (0.989)
  blocking collectives: 12.7 us -> 33.3 us
  waiting for transfers between devices: 38.1 us -> 26.9 us
  starting transfers between devices: 44.7 us -> 35.2 us
    all_to_all x0 -> x1, blocking collectives: none -> 20.6 us  [gathered(): lax.all_to_all(copies, 'mp', split_axis=0, concat_axis=0, tiled=True, axi...]
    all_to_all x1 -> x0, waiting for transfers between devices: 11.2 us -> none  [gathered(): lax.all_to_all(copies, 'mp', split_axis=0, concat_axis=0, tiled=True, axi...]
    all_to_all x1 -> x0, starting transfers between devices: 9.56 us -> none  [gathered(): lax.all_to_all(copies, 'mp', split_axis=0, concat_axis=0, tiled=True, axi...]
  transfers between devices with their start and end apart: 7 -> 6, of which waited for: 6 -> 5; matrix products, arithmetic and copies ran while one was open for 1% -> 1% of each run, Pallas kernels for 0% -> 0%
where the time goes in v10:
time: 99.9 us; the launch traced here: 99.5 us
  starting transfers between devices  35.2 us (35%)
  blocking collectives  33.3 us (33%)
  waiting for transfers between devices  26.9 us (27%)
  matrix products  1.46 us (1%)
  other arithmetic  1.36 us (1%)
  local copies, waits for them, and re-layouts  1.08 us (1%)
    ppermute x6, starting transfers between devices, moved(): return lax.ppermute(block, ('mp', 'intra'), perm)  35.2 us
    ppermute x6, waiting for transfers between devices, moved(): return lax.ppermute(block, ('mp', 'intra'), perm)  26.9 us
    all_to_all x1, blocking collectives, gathered(): lax.all_to_all(copies, 'mp', split_axis=0, concat_axis=0, tiled=True, axi...  20.6 us
    all_to_all x1, blocking collectives, reduced(): lax.all_to_all(second, 'inter', split_axis=0, concat_axis=0, tiled=True)  10.5 us
    all_gather x1, blocking collectives, gathered(): both = lax.all_gather(half, 'mp', axis_index_groups=pair)  2.17 us
  transfers between devices with their start and end apart: 6, of which 5 were waited for; matrix products, arithmetic and copies ran while one was open for 1% of the time, Pallas kernels for 0%

profile of v10, /device:TPU:64, one launch (start us, length us, event | category | flops | bytes accessed | tf_op | source)
XLA Modules:
  0.0 99.5 jit_solution(10171593971128927916)
XLA Ops:
  0.0 0.0 copy-start
  0.0 0.9 broadcast_in_dim.2
  0.9 20.6 %all_to_all.10 = bf16[8,32,512]{2,1,0:T(8,128)(2,1)S(1)} all-to-all(bf16[8,32,512]{2,1,0:T(8,128)(2,1)S(1)} %broadcast_in_dim.2), channel_id=1, replica_groups={{0,128,256,384,512,640,768,896},{64,192,320,448,576,704,832,960},{1,129..., dimensions={0} | all-to-all | bytes 524288 | tf_op jit(solution)/shard_map/all_to_all | solution.py:31
  21.5 2.2 %all-gather = bf16[16,32,512]{2,1,0:T(8,128)(2,1)S(1)} all-gather(bf16[8,32,512]{2,1,0:T(8,128)(2,1)S(1)} %all_to_all.10), channel_id=2, replica_groups={{0,64},{128,192},{256,320},{384,448},{512,576},{640,704},{768,832},{896..., dimensions={0}, use_global_device_ids=true | all-gather | bytes 786432 | tf_op jit(solution)/shard_map/all_gather | solution.py:34
  23.8 0.1 maximum_select_fusion
  23.9 0.2 fusion.1
  24.3 0.0 copy-done
  24.3 0.5 convolution_convert_fusion.1
  24.7 0.5 convolution_convert_fusion.2
  25.2 4.3 %collective-permute-start = (bf16[160,1792]{1,0:T(8,128)(2,1)S(1)}, bf16[160,1792]{1,0:T(8,128)(2,1)S(1)}, u32[]{:S(2)}, u32[]{:S(2)}) collective-permute-start(bf16[160,1792]{1,0:T(8,128)(2,1)S(1)} %convolution_convert_fusion.2), channel_id=1, source_target_pairs={{0,4},{4,8},{8,12},{12,16},{16,20},{20,24},{24,28},{28,32},{32,36}... | collective-permute-start | bytes 1720328 | tf_op jit(solution)/shard_map/ppermute | solution.py:52
  29.5 4.8 %collective-permute-start.1 = (bf16[160,1792]{1,0:T(8,128)(2,1)S(1)}, bf16[160,1792]{1,0:T(8,128)(2,1)S(1)}, u32[]{:S(2)}, u32[]{:S(2)}) collective-permute-start(bf16[160,1792]{1,0:T(8,128)(2,1)S(1)} %convolution_convert_fusion.1), channel_id=1, source_target_pairs={{0,60},{4,0},{8,4},{12,8},{16,12},{20,16},{24,20},{28,24},{32,28},... | collective-permute-start | bytes 1720328 | tf_op jit(solution)/shard_map/ppermute | solution.py:52
  34.3 0.5 fusion
  34.9 5.2 %collective-permute-done = bf16[160,1792]{1,0:T(8,128)(2,1)S(1)} collective-permute-done((bf16[160,1792]{1,0:T(8,128)(2,1)S(1)}, bf16[160,1792]{1,0:T(8,128)(2,1)S(1)}, u32[]{:S(2)}, u32[]{:S(2)}) %collective-permute-start) | collective-permute-done | bytes 573472 | tf_op jit(solution)/shard_map/ppermute | solution.py:52
  40.1 4.8 %collective-permute-done.1 = bf16[160,1792]{1,0:T(8,128)(2,1)S(1)} collective-permute-done((bf16[160,1792]{1,0:T(8,128)(2,1)S(1)}, bf16[160,1792]{1,0:T(8,128)(2,1)S(1)}, u32[]{:S(2)}, u32[]{:S(2)}) %collective-permute-start.1) | collective-permute-done | bytes 573472 | tf_op jit(solution)/shard_map/ppermute | solution.py:52
  44.9 0.1 convert_element_type.61
  45.0 0.1 convert_element_type.62
  45.1 0.1 fusion.8
  45.2 7.3 %collective-permute-start.2 = (bf16[64,1792]{1,0:T(8,128)(2,1)S(1)}, bf16[64,1792]{1,0:T(8,128)(2,1)S(1)}, u32[]{:S(2)}, u32[]{:S(2)}) collective-permute-start(bf16[64,1792]{1,0:T(8,128)(2,1)S(1)} %pad_maximum_fusion), channel_id=1, source_target_pairs={{0,12},{4,16},{8,20},{12,24},{16,28},{20,32},{24,36},{28,40},{32,4... | collective-permute-start | bytes 688136 | tf_op jit(solution)/shard_map/ppermute | solution.py:52
  52.5 9.2 %collective-permute-start.3 = (bf16[32,1792]{1,0:T(8,128)(2,1)S(1)}, bf16[32,1792]{1,0:T(8,128)(2,1)S(1)}, u32[]{:S(2)}, u32[]{:S(2)}) collective-permute-start(bf16[32,1792]{1,0:T(8,128)(2,1)S(1)} %get-tuple-element.30), channel_id=1, source_target_pairs={{0,52},{4,56},{8,60},{12,0},{16,4},{20,8},{24,12},{28,16},{32,20},... | collective-permute-start | bytes 344072 | tf_op jit(solution)/shard_map/ppermute | solution.py:52
  61.6 9.9 %collective-permute-done.3 = bf16[32,1792]{1,0:T(8,128)(2,1)S(1)} collective-permute-done((bf16[32,1792]{1,0:T(8,128)(2,1)S(1)}, bf16[32,1792]{1,0:T(8,128)(2,1)S(1)}, u32[]{:S(2)}, u32[]{:S(2)}) %collective-permute-start.3) | collective-permute-done | bytes 114720 | tf_op jit(solution)/shard_map/ppermute | solution.py:52
  71.5 0.0 collective-permute-done.2
  71.6 0.1 fusion.3
  71.6 4.0 %collective-permute-start.4 = (bf16[32,1792]{1,0:T(8,128)(2,1)S(1)}, bf16[32,1792]{1,0:T(8,128)(2,1)S(1)}, u32[]{:S(2)}, u32[]{:S(2)}) collective-permute-start(bf16[32,1792]{1,0:T(8,128)(2,1)S(1)} %get-tuple-element.33), channel_id=1, source_target_pairs={{0,16},{4,20},{8,24},{12,28},{16,32},{20,36},{24,40},{28,44},{32,4... | collective-permute-start | bytes 344072 | tf_op jit(solution)/shard_map/ppermute | solution.py:52
  75.7 5.6 %collective-permute-start.5 = (bf16[32,1792]{1,0:T(8,128)(2,1)S(1)}, bf16[32,1792]{1,0:T(8,128)(2,1)S(1)}, u32[]{:S(2)}, u32[]{:S(2)}) collective-permute-start(bf16[32,1792]{1,0:T(8,128)(2,1)S(1)} %get-tuple-element.34), channel_id=1, source_target_pairs={{0,52},{4,56},{8,60},{12,0},{16,4},{20,8},{24,12},{28,16},{32,20},... | collective-permute-start | bytes 344072 | tf_op jit(solution)/shard_map/ppermute | solution.py:52
  81.3 3.5 %collective-permute-done.4 = bf16[32,1792]{1,0:T(8,128)(2,1)S(1)} collective-permute-done((bf16[32,1792]{1,0:T(8,128)(2,1)S(1)}, bf16[32,1792]{1,0:T(8,128)(2,1)S(1)}, u32[]{:S(2)}, u32[]{:S(2)}) %collective-permute-start.4) | collective-permute-done | bytes 114720 | tf_op jit(solution)/shard_map/ppermute | solution.py:52
  84.8 3.4 %collective-permute-done.5 = bf16[32,1792]{1,0:T(8,128)(2,1)S(1)} collective-permute-done((bf16[32,1792]{1,0:T(8,128)(2,1)S(1)}, bf16[32,1792]{1,0:T(8,128)(2,1)S(1)}, u32[]{:S(2)}, u32[]{:S(2)}) %collective-permute-start.5) | collective-permute-done | bytes 114720 | tf_op jit(solution)/shard_map/ppermute | solution.py:52
  88.2 0.1 fusion.11
  88.3 10.5 %all_to_all.11 = bf16[4,8,1792]{2,1,0:T(8,128)(2,1)S(1)} all-to-all(bf16[4,8,1792]{2,1,0:T(8,128)(2,1)S(1)} %fusion.11), channel_id=1, replica_groups=mesh['mp'=16,'intra'=16,'inter'=4] {'inter'}, dimensions={0} | all-to-all | bytes 229376 | tf_op jit(solution)/shard_map/all_to_all | solution.py:88
  98.9 0.6 convert_reduce_fusion
  (13 shorter events, 0.2 us)
Async XLA Ops:
  0.0 24.3 %copy-start = (bf16[512,1792]{1,0:T(8,128)(2,1)S(1)}, bf16[512,1792]{1,0:T(8,128)(2,1)}, u32[]{:S(2)}) copy-start(bf16[512,1792]{1,0:T(8,128)(2,1)} %param.3) | copy-start | bytes 5505028
  25.2 14.9 %collective-permute-start = (bf16[160,1792]{1,0:T(8,128)(2,1)S(1)}, bf16[160,1792]{1,0:T(8,128)(2,1)S(1)}, u32[]{:S(2)}, u32[]{:S(2)}) collective-permute-start(bf16[160,1792]{1,0:T(8,128)(2,1)S(1)} %convolution_convert_fusion.2), channel_id=1, source_target_pairs={{0,4},{4,8},{8,12},{12,16},{16,20},{20,24},{24,28},{28,32},{32,36}... | collective-permute-start | bytes 1720328 | tf_op jit(solution)/shard_map/ppermute | solution.py:52
  29.5 15.4 %collective-permute-start.1 = (bf16[160,1792]{1,0:T(8,128)(2,1)S(1)}, bf16[160,1792]{1,0:T(8,128)(2,1)S(1)}, u32[]{:S(2)}, u32[]{:S(2)}) collective-permute-start(bf16[160,1792]{1,0:T(8,128)(2,1)S(1)} %convolution_convert_fusion.1), channel_id=1, source_target_pairs={{0,60},{4,0},{8,4},{12,8},{16,12},{20,16},{24,20},{28,24},{32,28},... | collective-permute-start | bytes 1720328 | tf_op jit(solution)/shard_map/ppermute | solution.py:52
  45.2 26.3 %collective-permute-start.2 = (bf16[64,1792]{1,0:T(8,128)(2,1)S(1)}, bf16[64,1792]{1,0:T(8,128)(2,1)S(1)}, u32[]{:S(2)}, u32[]{:S(2)}) collective-permute-start(bf16[64,1792]{1,0:T(8,128)(2,1)S(1)} %pad_maximum_fusion), channel_id=1, source_target_pairs={{0,12},{4,16},{8,20},{12,24},{16,28},{20,32},{24,36},{28,40},{32,4... | collective-permute-start | bytes 688136 | tf_op jit(solution)/shard_map/ppermute | solution.py:52
  52.5 19.1 %collective-permute-start.3 = (bf16[32,1792]{1,0:T(8,128)(2,1)S(1)}, bf16[32,1792]{1,0:T(8,128)(2,1)S(1)}, u32[]{:S(2)}, u32[]{:S(2)}) collective-permute-start(bf16[32,1792]{1,0:T(8,128)(2,1)S(1)} %get-tuple-element.30), channel_id=1, source_target_pairs={{0,52},{4,56},{8,60},{12,0},{16,4},{20,8},{24,12},{28,16},{32,20},... | collective-permute-start | bytes 344072 | tf_op jit(solution)/shard_map/ppermute | solution.py:52
  71.6 13.2 %collective-permute-start.4 = (bf16[32,1792]{1,0:T(8,128)(2,1)S(1)}, bf16[32,1792]{1,0:T(8,128)(2,1)S(1)}, u32[]{:S(2)}, u32[]{:S(2)}) collective-permute-start(bf16[32,1792]{1,0:T(8,128)(2,1)S(1)} %get-tuple-element.33), channel_id=1, source_target_pairs={{0,16},{4,20},{8,24},{12,28},{16,32},{20,36},{24,40},{28,44},{32,4... | collective-permute-start | bytes 344072 | tf_op jit(solution)/shard_map/ppermute | solution.py:52
  75.7 12.5 %collective-permute-start.5 = (bf16[32,1792]{1,0:T(8,128)(2,1)S(1)}, bf16[32,1792]{1,0:T(8,128)(2,1)S(1)}, u32[]{:S(2)}, u32[]{:S(2)}) collective-permute-start(bf16[32,1792]{1,0:T(8,128)(2,1)S(1)} %get-tuple-element.34), channel_id=1, source_target_pairs={{0,52},{4,56},{8,60},{12,0},{16,4},{20,8},{24,12},{28,16},{32,20},... | collective-permute-start | bytes 344072 | tf_op jit(solution)/shard_map/ppermute | solution.py:52
